TPU v7x, 256 devices: a whole 4x4x8 slice. The times are simulated.
256 devices in a mesh: mem: 32 (over z, x), head: 8 (over y, core).
Axes of the slice: x: 4, y: 4, z: 8, core: 2. Of those that a mesh axis runs over, the one named last changes fastest.
Arguments:
- query_rows: bfloat16 [32, 1024, 4096], P('mem', 'head'), may hold values from -6 to 6
- key_rows: bfloat16 [32, 1024, 4096], P('mem', 'head'), may hold values from -6 to 6
- value_rows: bfloat16 [32, 1024, 4096], P('mem', 'head'), may hold values from -6 to 6
- memory_keys: bfloat16 [256, 128, 4096], P('mem', None, 'head'), may hold values from -6 to 6
- memory_values: bfloat16 [256, 128, 4096], P('mem', None, 'head'), may hold values from -6 to 6
- owner_list: int32 [32, 8, 2], P('mem'), may hold values from 0 to 31, all different within a row; in each aligned block of 8 rows (0 to 7, 8 to 15, ..., all dimensions but the last counted through in order) at most 2 rows name the same one
- slot_list: int32 [32, 8, 2], P('mem'), may hold values from 0 to 7
- gate_logit: float32 [32], P('head'), may hold values from -2 to 2
Outputs:
- mixed_out: bfloat16 [32, 1024, 4096], P('mem', 'head')
Inputs may be any that keep to these rules, and one draw needn't show every extreme that they name: `owner_list`: the 2 entries of one query block name different indices; among the 8 query blocks of one segment, no index is named more than 2 times.
All inputs are finite; a program needn't handle non-finite values.
Results may differ from a plain program's by a relative error of at most 0.012.
Values may be sent and summed in bfloat16 or wider, within the bound.
No kernel may reach another device: no remote copies, remote signals or barrier semaphores. Data moves between devices by JAX's collectives and lax.ppermute only.
A program may use at most 128 MiB of HBM per device.

v0:
```python
import jax
import jax.numpy as jnp
from jax import lax
from jax.sharding import PartitionSpec as P

DH = 128
BLK = 128
TOPK = 2
CAP = 2


negative_fill = -1e30


def local_attend(query_heads, key_heads, value_heads):
    length = query_heads.shape[0]
    block_rows = min(512, length)
    scaling = query_heads.shape[2] ** (-0.5)

    def one_block(number):
        offset = number * block_rows
        query_block = lax.dynamic_slice_in_dim(query_heads, offset, block_rows, 0)
        scores = (
            jnp.einsum("qhd,khd->hqk", query_block, key_heads, preferred_element_type=jnp.float32)
            * scaling
        )
        positions = offset + jnp.arange(block_rows, dtype=jnp.int32)
        allowed = jnp.arange(length, dtype=jnp.int32)[None, :] <= positions[:, None]
        scores = jnp.where(allowed[None], scores, negative_fill)
        weights = jax.nn.softmax(scores, axis=-1).astype(jnp.bfloat16)
        return jnp.einsum("hqk,khd->qhd", weights, value_heads, preferred_element_type=jnp.float32)

    pieces = lax.map(one_block, jnp.arange(length // block_rows, dtype=jnp.int32))
    return pieces.reshape(query_heads.shape)


def request_ranks(owner_ids):
    total_count = owner_ids.shape[-1]
    positions = jnp.arange(total_count, dtype=jnp.int32)
    matched = owner_ids[..., None, :] == owner_ids[..., :, None]
    earlier = matched & (positions[None, :] < positions[:, None])
    return jnp.sum(earlier.astype(jnp.int32), axis=-1)


def on_device(
    query_rows, key_rows, value_rows, memory_keys, memory_values, owner_list, slot_list, gate_logit
):
    query_cols, key_cols, value_cols = (
        lax.all_to_all(query_rows, "head", split_axis=2, concat_axis=1, tiled=True),
        lax.all_to_all(key_rows, "head", split_axis=2, concat_axis=1, tiled=True),
        lax.all_to_all(value_rows, "head", split_axis=2, concat_axis=1, tiled=True),
    )
    length = query_cols.shape[1]
    width = query_cols.shape[2]
    head_count = width // DH
    query_heads = query_cols[0].reshape(length, head_count, DH)
    key_heads = key_cols[0].reshape(length, head_count, DH)
    value_heads = value_cols[0].reshape(length, head_count, DH)
    local_part = local_attend(query_heads, key_heads, value_heads)
    mem_count = lax.axis_size("mem")
    query_count = owner_list.shape[1]
    owner_ids = owner_list[0].reshape(-1)
    slot_ids = slot_list[0].reshape(-1)
    ranking = request_ranks(owner_ids)
    owner_range = jnp.arange(mem_count, dtype=jnp.int32)
    cap_range = jnp.arange(CAP, dtype=jnp.int32)
    owner_hot = (owner_ids[:, None] == owner_range[None, :]).astype(jnp.int32)
    rank_hot = (ranking[:, None] == cap_range[None, :]).astype(jnp.int32)
    outgoing = jnp.sum(
        owner_hot[:, :, None] * rank_hot[:, None, :] * slot_ids[:, None, None], axis=0
    )
    wanted = lax.all_to_all(outgoing, "mem", split_axis=0, concat_axis=0, tiled=True)
    outgoing_keys = memory_keys[wanted]
    outgoing_values = memory_values[wanted]
    fetched_keys, fetched_values = (
        lax.all_to_all(outgoing_keys, "mem", split_axis=0, concat_axis=0, tiled=True),
        lax.all_to_all(outgoing_values, "mem", split_axis=0, concat_axis=0, tiled=True),
    )
    flat_index = owner_ids * CAP + ranking
    fetched_keys = fetched_keys.reshape(mem_count * CAP, BLK, width)[flat_index]
    fetched_values = fetched_values.reshape(mem_count * CAP, BLK, width)[flat_index]
    key_blocks = fetched_keys.reshape(query_count, TOPK * BLK, head_count, DH)
    value_blocks = fetched_values.reshape(query_count, TOPK * BLK, head_count, DH)
    query_blocks = query_heads.reshape(query_count, BLK, head_count, DH)
    scaling = DH ** (-0.5)
    memory_scores = (
        jnp.einsum("bqhd,bkhd->bhqk", query_blocks, key_blocks, preferred_element_type=jnp.float32)
        * scaling
    )
    memory_weights = jax.nn.softmax(memory_scores, axis=-1).astype(jnp.bfloat16)
    memory_part = jnp.einsum(
        "bhqk,bkhd->bqhd", memory_weights, value_blocks, preferred_element_type=jnp.float32
    )
    memory_part = memory_part.reshape(length, head_count, DH)
    gating = jax.nn.sigmoid(gate_logit)[None, :, None]
    combined = gating * memory_part + (1.0 - gating) * local_part
    mixed_cols = combined.reshape(1, length, width).astype(jnp.bfloat16)
    return lax.all_to_all(mixed_cols, "head", split_axis=1, concat_axis=2, tiled=True)


def solution(mesh):
    placed = (
        P("mem", "head", None),
        P("mem", "head", None),
        P("mem", "head", None),
        P("mem", None, "head"),
        P("mem", None, "head"),
        P("mem", None, None),
        P("mem", None, None),
        P("head"),
    )
    return jax.shard_map(
        on_device, mesh=mesh, in_specs=placed, out_specs=P("mem", "head", None), check_vma=False
    )
```

profile of v0, /device:TPU:102, one launch (start us, length us, event | category | flops | bytes accessed | tf_op | source)
XLA Modules:
  0.0 595.1 jit_solution(2170204665150012628)
XLA Ops:
  2.8 10.2 %all-to-all-start = ((s32[32,1,2]{2,1,0:T(1,128)}), s32[32,1,2]{2,1,0:T(1,128)S(1)}, u32[]{:S(2)}, u32[]{:S(2)}) async-start(s32[32,1,2]{2,1,0:T(1,128)} %copy.112), calls=%async_computation | async-start | bytes 32768 | tf_op jit(solution)/shard_map/all_to_all | solution.py:72
  13.0 5.0 copy.118
  18.6 23.3 %reduce = bf16[4096,128]{1,0:T(8,128)(2,1)} reduce(bf16[4096,1,128]{2,1,0:T(2,128)(2,1)S(1)} %bitcast.99, bf16[]{:T(256)} %broadcast.180), dimensions={1}, to_apply=%bitcast.69.reduce_sub_computation | reduce | bytes 2097154
  44.1 4.5 all-to-all-start.3
  48.6 5.0 copy.125
  53.6 23.3 %reduce.1 = bf16[4096,128]{1,0:T(8,128)(2,1)} reduce(bf16[4096,1,128]{2,1,0:T(2,128)(2,1)S(1)} %bitcast.101, bf16[]{:T(256)} %broadcast.180), dimensions={1}, to_apply=%bitcast.71.reduce_sub_computation | reduce | bytes 2097154
  79.1 5.3 all-to-all-start.4
  84.5 5.0 copy.127
  89.5 23.3 %reduce.2 = bf16[4096,128]{1,0:T(8,128)(2,1)} reduce(bf16[4096,1,128]{2,1,0:T(2,128)(2,1)S(1)} %bitcast.102, bf16[]{:T(256)} %broadcast.180), dimensions={1}, to_apply=%bitcast.73.reduce_sub_computation | reduce | bytes 2097154
  115.0 4.8 all-to-all-start.5
  120.1 5.3 gather_fusion.2
  125.5 10.3 %all-to-all-done.5 = bf16[8,2,32768]{2,1,0:T(2,128)(2,1)S(1)} async-done(((bf16[8,2,32768]{2,1,0:T(2,128)(2,1)}), bf16[8,2,32768]{2,1,0:T(2,128)(2,1)S(1)}, u32[]{:S(2)}, u32[]{:S(2)}) %all-to-all-start.5) | async-done | bytes 1048608 | tf_op jit(solution)/shard_map/all_to_all | solution.py:51
  136.8 9.8 %all-to-all-start.2 = ((bf16[32,2,128,512]{3,2,1,0:T(8,128)(2,1)}), bf16[32,2,128,512]{3,2,1,0:T(8,128)(2,1)}, u32[]{:S(2)}, u32[]{:S(2)}) async-start(bf16[32,2,128,512]{3,2,1,0:T(8,128)(2,1)} %bitcast.92), calls=%async_computation.2 | async-start | bytes 16777216 | tf_op jit(solution)/shard_map/all_to_all | solution.py:76
  146.6 5.3 gather_fusion
  151.9 183.6 %all-to-all-done.2 = bf16[32,2,128,512]{3,2,1,0:T(8,128)(2,1)} async-done(((bf16[32,2,128,512]{3,2,1,0:T(8,128)(2,1)}), bf16[32,2,128,512]{3,2,1,0:T(8,128)(2,1)}, u32[]{:S(2)}, u32[]{:S(2)}) %all-to-all-start.2) | async-done | bytes 8388640 | tf_op jit(solution)/shard_map/all_to_all | solution.py:76
  335.6 9.5 %all-to-all-start.1 = ((bf16[32,2,128,512]{3,2,1,0:T(8,128)(2,1)}), bf16[32,2,128,512]{3,2,1,0:T(8,128)(2,1)}, u32[]{:S(2)}, u32[]{:S(2)}) async-start(bf16[32,2,128,512]{3,2,1,0:T(8,128)(2,1)} %bitcast.91), calls=%async_computation.1 | async-start | bytes 16777216 | tf_op jit(solution)/shard_map/all_to_all | solution.py:77
  345.4 4.3 reshape.282
  351.8 4.3 reshape.284
  358.7 4.3 reshape.286
  365.7 69.3 %while.10 = (s32[]{:T(128)}, f32[2,512,4,128]{1,0,3,2:T(2,128)}, s32[2]{0:T(128)S(1)}, bf16[1024,4,128]{0,2,1:T(8,128)(2,1)}, bf16[1024,4,128]{2,0,1:T(8,128)(2,...) while((s32[]{:T(128)}, f32[2,512,4,128]{1,0,3,2:T(2,128)}, ...), condition=%wide.region_7.8_spmd, body=%wide.region_4.7_spmd.sunk | while | flops 1086850560 | bytes 25710764 | solution.py:33
  367.3 7.9 %fusion.58 = (f32[4,512]{1,0:T(4,128)S(1)}, f32[4,512,1024]{2,1,0:T(8,128)}) fusion(pred[512,1024]{1,0:T(8,128)(4,1)S(1)} %iota_compare_fusion.4, bf16[1024,4,128]{2,0,1:T(8,128)(2,1)} %get-tuple-element.153, bf16[1024,4,128]{0,2,1:T(8,128)(2,1)} %get-tuple-element.152, s32[]{:T(128)S(6)} %select_n.48), kind=kOutput, calls=%fused_computation.57.clone.1 | convolution fusion | flops 545260544 | bytes 10493956 | tf_op jit(solution)/shard_map/while/body/eval_jaxpr/sub | solution.py:30
  375.2 4.9 fusion.59
  380.9 19.5 %dynamic_update_slice.5 = f32[2,512,4,128]{1,0,3,2:T(2,128)} dynamic-update-slice(f32[2,512,4,128]{1,0,3,2:T(2,128)} %get-tuple-element.140, f32[1,512,4,128]{1,0,3,2:T(1,128)S(1)} %copy.160, s32[]{:T(128)} %get-tuple-element.139, s32[]{:T(128)} %constant.5.clone.1..sunk, s32[]{:T(128)} %constant.5.clone.1..sunk, s32[]{:T(128)} %constant.5.clone.1..sunk) | dynamic-update-slice | bytes 2097156 | tf_op jit(solution)/shard_map/while/body/jit(dynamic_update_index_in_dim)/dynamic_update_slice | solution.py:33
  402.0 7.9 %fusion.58 = (f32[4,512]{1,0:T(4,128)S(1)}, f32[4,512,1024]{2,1,0:T(8,128)}) fusion(pred[512,1024]{1,0:T(8,128)(4,1)S(1)} %iota_compare_fusion.4, bf16[1024,4,128]{2,0,1:T(8,128)(2,1)} %get-tuple-element.153, bf16[1024,4,128]{0,2,1:T(8,128)(2,1)} %get-tuple-element.152, s32[]{:T(128)S(6)} %select_n.48), kind=kOutput, calls=%fused_computation.57.clone.1 | convolution fusion | flops 545260544 | bytes 10493956 | tf_op jit(solution)/shard_map/while/body/eval_jaxpr/sub | solution.py:30
  409.8 4.9 fusion.59
  415.5 19.5 %dynamic_update_slice.5 = f32[2,512,4,128]{1,0,3,2:T(2,128)} dynamic-update-slice(f32[2,512,4,128]{1,0,3,2:T(2,128)} %get-tuple-element.140, f32[1,512,4,128]{1,0,3,2:T(1,128)S(1)} %copy.160, s32[]{:T(128)} %get-tuple-element.139, s32[]{:T(128)} %constant.5.clone.1..sunk, s32[]{:T(128)} %constant.5.clone.1..sunk, s32[]{:T(128)} %constant.5.clone.1..sunk) | dynamic-update-slice | bytes 2097156 | tf_op jit(solution)/shard_map/while/body/jit(dynamic_update_index_in_dim)/dynamic_update_slice | solution.py:33
  435.0 4.0 reshape.280
  439.0 5.4 gather_fusion.3
  450.8 83.0 %all-to-all-done.1 = bf16[32,2,128,512]{3,2,1,0:T(8,128)(2,1)} async-done(((bf16[32,2,128,512]{3,2,1,0:T(8,128)(2,1)}), bf16[32,2,128,512]{3,2,1,0:T(8,128)(2,1)}, u32[]{:S(2)}, u32[]{:S(2)}) %all-to-all-start.1) | async-done | bytes 8388640 | tf_op jit(solution)/shard_map/all_to_all | solution.py:77
  533.9 4.1 gather_fusion.1
  552.9 7.0 %reduce.3 = bf16[1024,512]{1,0:T(8,128)(2,1)S(1)} reduce(bf16[1024,1,512]{2,1,0:T(2,128)(2,1)S(1)} %bitcast.100, bf16[]{:T(256)} %broadcast.180), dimensions={1}, to_apply=%bitcast.75.reduce_sub_computation | reduce | bytes 2097154
  560.7 28.9 %all_to_all.85 = bf16[8,2,32768]{2,1,0:T(2,128)(2,1)S(1)} all-to-all(bf16[8,2,32768]{2,1,0:T(2,128)(2,1)S(1)} %reshape.287), channel_id=1, replica_groups=mesh['mem'=32,'head'=8] {'head'}, dimensions={0} | all-to-all | bytes 2097152 | tf_op jit(solution)/shard_map/all_to_all | solution.py:98
  (77 shorter events, 49.6 us)
Async XLA Ops:
  0.0 120.1 %copy-start = (bf16[8,128,512]{2,1,0:T(8,128)(2,1)S(1)}, bf16[8,128,512]{2,1,0:T(8,128)(2,1)}, u32[]{:S(2)}) copy-start(bf16[8,128,512]{2,1,0:T(8,128)(2,1)} %param.13) | copy-start | bytes 3145732
  2.8 41.3 %all-to-all-start = ((s32[32,1,2]{2,1,0:T(1,128)}), s32[32,1,2]{2,1,0:T(1,128)S(1)}, u32[]{:S(2)}, u32[]{:S(2)}) async-start(s32[32,1,2]{2,1,0:T(1,128)} %copy.112), calls=%async_computation | async-start | bytes 32768 | tf_op jit(solution)/shard_map/all_to_all | solution.py:72
  44.1 35.1 %all-to-all-start.3 = ((bf16[8,2,32768]{2,1,0:T(2,128)(2,1)}), bf16[8,2,32768]{2,1,0:T(2,128)(2,1)}, u32[]{:S(2)}, u32[]{:S(2)}) async-start(bf16[8,2,32768]{2,1,0:T(2,128)(2,1)} %reshape.281), calls=%async_computation.3 | async-start | bytes 2097152 | tf_op jit(solution)/shard_map/all_to_all | solution.py:49
  79.1 35.9 %all-to-all-start.4 = ((bf16[8,2,32768]{2,1,0:T(2,128)(2,1)}), bf16[8,2,32768]{2,1,0:T(2,128)(2,1)}, u32[]{:S(2)}, u32[]{:S(2)}) async-start(bf16[8,2,32768]{2,1,0:T(2,128)(2,1)} %reshape.283), calls=%async_computation.4 | async-start | bytes 2097152 | tf_op jit(solution)/shard_map/all_to_all | solution.py:50
  115.0 20.8 %all-to-all-start.5 = ((bf16[8,2,32768]{2,1,0:T(2,128)(2,1)}), bf16[8,2,32768]{2,1,0:T(2,128)(2,1)S(1)}, u32[]{:S(2)}, u32[]{:S(2)}) async-start(bf16[8,2,32768]{2,1,0:T(2,128)(2,1)} %reshape.285), calls=%async_computation.5 | async-start | bytes 2097152 | tf_op jit(solution)/shard_map/all_to_all | solution.py:51
  135.8 1.0 copy-start.4
  135.8 10.8 %copy-start.2 = (bf16[8,128,512]{2,1,0:T(8,128)(2,1)S(1)}, bf16[8,128,512]{2,1,0:T(8,128)(2,1)}, u32[]{:S(2)}) copy-start(bf16[8,128,512]{2,1,0:T(8,128)(2,1)} %param.14) | copy-start | bytes 3145732
  136.8 198.8 %all-to-all-start.2 = ((bf16[32,2,128,512]{3,2,1,0:T(8,128)(2,1)}), bf16[32,2,128,512]{3,2,1,0:T(8,128)(2,1)}, u32[]{:S(2)}, u32[]{:S(2)}) async-start(bf16[32,2,128,512]{3,2,1,0:T(8,128)(2,1)} %bitcast.92), calls=%async_computation.2 | async-start | bytes 16777216 | tf_op jit(solution)/shard_map/all_to_all | solution.py:76
  335.6 9.5 %copy-start.5 = (s32[1,8,2]{1,2,0:T(2,128)S(1)}, s32[1,8,2]{1,2,0:T(2,128)}, u32[]{:S(2)}) copy-start(s32[1,8,2]{1,2,0:T(2,128)} %param.15) | copy-start | bytes 196
  335.6 9.7 %copy-start.6 = (f32[4]{0:T(128)S(1)}, f32[4]{0:T(128)}, u32[]{:S(2)}) copy-start(f32[4]{0:T(128)} %param.17) | copy-start | bytes 52
  335.6 198.3 %all-to-all-start.1 = ((bf16[32,2,128,512]{3,2,1,0:T(8,128)(2,1)}), bf16[32,2,128,512]{3,2,1,0:T(8,128)(2,1)}, u32[]{:S(2)}, u32[]{:S(2)}) async-start(bf16[32,2,128,512]{3,2,1,0:T(8,128)(2,1)} %bitcast.91), calls=%async_computation.1 | async-start | bytes 16777216 | tf_op jit(solution)/shard_map/all_to_all | solution.py:77
  546.2 2.9 copy-start.3
  591.9 3.0 copy-start.1
where the time goes:
time: 607 us; the launch traced here: 595 us
  waiting for transfers between devices  277 us (46%)
  local copies, waits for them, and re-layouts  130 us (21%)
  other arithmetic  83.1 us (14%)
  starting transfers between devices  44.1 us (7%)
  matrix products  30 us (5%)
  blocking collectives  28.9 us (5%)
    all_to_all x1, waiting for transfers between devices, on_device(): lax.all_to_all(outgoing_keys, 'mem', split_axis=0, concat_axis=0, tiled=T...  184 us
    all_to_all x1, waiting for transfers between devices, on_device(): lax.all_to_all(outgoing_values, 'mem', split_axis=0, concat_axis=0, tiled...  83 us
    unnamed x4, other arithmetic  77.1 us
    unnamed x32, local copies, waits for them, and re-layouts  41.1 us
    dynamic_update_slice x4, local copies, waits for them, and re-layouts, local_attend(): lax.map(one_block, jnp.arange(length // block_rows, dtype=jnp.int32))  40.4 us
    all_to_all x1, blocking collectives, on_device(): lax.all_to_all(mixed_cols, 'head', split_axis=1, concat_axis=2, tiled=True)  28.9 us
    sub x2, matrix products, one_block(): weights = jax.nn.softmax(scores, axis=-1).astype(jnp.bfloat16)  15.7 us
  transfers between devices with their start and end apart: 6, of which 3 were waited for; matrix products, arithmetic and copies ran while one was open for 35% of the time, Pallas kernels for 0%

commit v1 on v0

v1 whole, which is shorter than its diff:
```python
import functools
import math

import jax
import jax.numpy as jnp
from jax import lax
from jax.experimental import pallas as pl
from jax.experimental.pallas import tpu as pltpu
from jax.sharding import PartitionSpec as P

DH = 128
BLK = 128
HEADS_DEV = 4
HEAD_DEVS = 8
MEM_DEVS = 32
SLOTS = 8
ROWS = 16
WIDTH = HEADS_DEV * DH
Q_TILE = 256
EXP_SCALE = math.log2(math.e) / math.sqrt(DH)
MASKED = -1e30

VMEM = pl.BlockSpec(memory_space=pltpu.VMEM)
SMEM = pl.BlockSpec(memory_space=pltpu.SMEM)


def params(mib):
    return pltpu.CompilerParams(vmem_limit_bytes=mib * 1024 * 1024)


def dot_nt(a, b):
    return lax.dot_general(a, b, (((1,), (1,)), ((), ())), preferred_element_type=jnp.float32)


def spread_kernel(keys_ref, values_ref, ids_ref, out_ref):
    for dest in range(MEM_DEVS):
        z, x = dest // HEADS_DEV, dest % HEADS_DEV
        rows, cols = pl.ds(z * ROWS, ROWS), pl.ds(x * DH, DH)
        out_ref[dest, 0:SLOTS] = keys_ref[:, rows, cols]
        out_ref[dest, SLOTS : 2 * SLOTS] = values_ref[:, rows, cols]
        out_ref[dest, 2 * SLOTS] = ids_ref[...]


def gather_kernel(ids_ref, table_ref, out_ref):
    def one(dest, carry):
        for k in range(2):
            block = ids_ref[2 * dest + k]
            owner, slot = block // SLOTS, block % SLOTS
            out_ref[dest, k, 0] = table_ref[owner, slot]
            out_ref[dest, k, 1] = table_ref[owner, SLOTS + slot]
        return carry

    lax.fori_loop(0, MEM_DEVS * HEAD_DEVS, one, 0, unroll=8)


def pack_kernel(me_ref, q_ref, k_ref, v_ref, *out_refs):
    for shift in range(HEAD_DEVS):
        dest = (me_ref[0] + shift) % HEAD_DEVS
        cols = pl.ds(pl.multiple_of(dest * WIDTH, WIDTH), WIDTH)
        for i, ref in enumerate((q_ref, k_ref, v_ref)):
            out_refs[shift][i] = ref[:, cols]


def local_kernel(me_ref, gate_ref, *refs):
    ins, outs = refs[:HEAD_DEVS], refs[HEAD_DEVS : 2 * HEAD_DEVS]
    held, result = refs[2 * HEAD_DEVS :]
    me = me_ref[0]
    for shift in range(HEAD_DEVS):
        held[:, (me + HEAD_DEVS - shift) % HEAD_DEVS] = ins[shift][...]
    length = HEAD_DEVS * BLK
    blocks = Q_TILE // BLK
    parts = []
    for j in range(HEADS_DEV):
        cols = pl.ds(j * DH, DH)
        gate = jax.nn.sigmoid(jnp.full((1, DH), gate_ref[j], jnp.float32))
        high = gate.astype(jnp.bfloat16)
        rest = gate - high.astype(jnp.float32)
        mid = rest.astype(jnp.bfloat16)
        low = (rest - mid.astype(jnp.float32)).astype(jnp.bfloat16)
        parts.append((high, mid, low))
        for tile in range(length // Q_TILE):
            rows = pl.ds(tile * blocks, blocks)
            query = held[0, rows, :, cols].reshape(Q_TILE, DH)
            diag = dot_nt(query, held[1, rows, :, cols].reshape(Q_TILE, DH))
            row_ids = lax.broadcasted_iota(jnp.int32, (Q_TILE, Q_TILE), 0)
            col_ids = lax.broadcasted_iota(jnp.int32, (Q_TILE, Q_TILE), 1)
            diag = jnp.where(col_ids <= row_ids, diag, MASKED)
            top = jnp.max(diag, axis=1, keepdims=True)
            if tile:
                before = pl.ds(0, tile * blocks)
                off = dot_nt(query, held[1, before, :, cols].reshape(tile * Q_TILE, DH))
                top = jnp.maximum(top, jnp.max(off, axis=1, keepdims=True))
            weights = jnp.exp2((diag - top) * EXP_SCALE)
            total = jnp.sum(weights, axis=1, keepdims=True)
            part = jnp.dot(
                weights.astype(jnp.bfloat16),
                held[2, rows, :, cols].reshape(Q_TILE, DH),
                preferred_element_type=jnp.float32,
            )
            if tile:
                weights = jnp.exp2((off - top) * EXP_SCALE)
                total = total + jnp.sum(weights, axis=1, keepdims=True)
                part = part + jnp.dot(
                    weights.astype(jnp.bfloat16),
                    held[2, before, :, cols].reshape(tile * Q_TILE, DH),
                    preferred_element_type=jnp.float32,
                )
            part = part * ((1.0 - gate) / total)
            result[rows, pl.ds(j * BLK, BLK), :] = part.astype(jnp.bfloat16).reshape(
                blocks, BLK, DH
            )
    tail = jnp.concatenate(
        [parts[j][i] for i in range(3) for j in range(HEADS_DEV)]
        + [jnp.zeros((ROWS - 3 * HEADS_DEV, DH), jnp.bfloat16)],
        axis=0,
    )
    for shift in range(HEAD_DEVS):
        outs[shift][pl.ds(0, WIDTH), :] = result[(me + shift) % HEAD_DEVS]
        outs[shift][pl.ds(WIDTH, ROWS), :] = tail


def mix_kernel(me_ref, q_ref, fetched_ref, *refs):
    ins, out_ref = refs[:HEAD_DEVS], refs[HEAD_DEVS]
    for shift in range(HEAD_DEVS):
        owner = (me_ref[0] + HEAD_DEVS - shift) % HEAD_DEVS
        tail = ins[shift][pl.ds(WIDTH, ROWS), :].astype(jnp.float32)
        for j in range(HEADS_DEV):
            cols = pl.ds(pl.multiple_of(owner * WIDTH + j * DH, DH), DH)
            keys = fetched_ref[:, j, owner, :, 0].reshape(2 * BLK, DH)
            values = fetched_ref[:, j, owner, :, 1].reshape(2 * BLK, DH)
            scores = dot_nt(q_ref[:, cols], keys)
            top = jnp.max(scores, axis=1, keepdims=True)
            weights = jnp.exp2((scores - top) * EXP_SCALE)
            total = jnp.sum(weights, axis=1, keepdims=True)
            part = jnp.dot(weights.astype(jnp.bfloat16), values, preferred_element_type=jnp.float32)
            gate = tail[j : j + 1] + tail[4 + j : 5 + j] + tail[8 + j : 9 + j]
            local = ins[shift][pl.ds(j * BLK, BLK), :].astype(jnp.float32)
            out_ref[:, cols] = (part * (gate / total) + local).astype(jnp.bfloat16)


def on_device(
    query_rows, key_rows, value_rows, memory_keys, memory_values, owner_list, slot_list, gate_logit
):
    me = lax.axis_index("head").astype(jnp.int32).reshape(1)

    def rotated(arrays):
        return [arrays[0]] + [
            lax.ppermute(
                arrays[s], "head", [(i, (i + s) % HEAD_DEVS) for i in range(HEAD_DEVS)]
            )
            for s in range(1, HEAD_DEVS)
        ]

    ids = (owner_list * SLOTS + slot_list).reshape(ROWS, 1)
    ids = jnp.broadcast_to(ids.astype(jnp.bfloat16), (ROWS, DH))
    spread = pl.pallas_call(
        spread_kernel,
        out_shape=jax.ShapeDtypeStruct((MEM_DEVS, 2 * SLOTS + 1, ROWS, DH), jnp.bfloat16),
        in_specs=[VMEM] * 3,
        out_specs=VMEM,
        compiler_params=params(24),
    )(memory_keys, memory_values, ids)
    table = lax.all_to_all(spread, "mem", split_axis=0, concat_axis=0, tiled=True)

    packed = pl.pallas_call(
        pack_kernel,
        out_shape=[jax.ShapeDtypeStruct((3, BLK, WIDTH), jnp.bfloat16)] * HEAD_DEVS,
        in_specs=[SMEM] + [VMEM] * 3,
        out_specs=[VMEM] * HEAD_DEVS,
        compiler_params=params(24),
    )(me, query_rows[0], key_rows[0], value_rows[0])
    packed = rotated(packed)
    local = pl.pallas_call(
        local_kernel,
        out_shape=[jax.ShapeDtypeStruct((WIDTH + ROWS, DH), jnp.bfloat16)] * HEAD_DEVS,
        in_specs=[SMEM, SMEM] + [VMEM] * HEAD_DEVS,
        out_specs=[VMEM] * HEAD_DEVS,
        scratch_shapes=[
            pltpu.VMEM((3, HEAD_DEVS, BLK, WIDTH), jnp.bfloat16),
            pltpu.VMEM((HEAD_DEVS, WIDTH, DH), jnp.bfloat16),
        ],
        compiler_params=params(32),
    )(me, gate_logit, *packed)
    local = rotated(local)

    all_ids = table[:, 2 * SLOTS, :, 0].astype(jnp.int32).reshape(MEM_DEVS * ROWS)
    requested = pl.pallas_call(
        gather_kernel,
        out_shape=jax.ShapeDtypeStruct((MEM_DEVS * HEAD_DEVS, 2, 2, ROWS, DH), jnp.bfloat16),
        in_specs=[SMEM, VMEM],
        out_specs=VMEM,
        compiler_params=params(24),
    )(all_ids, table)
    fetched = lax.all_to_all(requested, ("mem", "head"), split_axis=0, concat_axis=0, tiled=True)
    fetched = fetched.reshape(BLK // ROWS, HEADS_DEV, HEAD_DEVS, 2, 2, ROWS, DH)
    mixed = pl.pallas_call(
        mix_kernel,
        out_shape=jax.ShapeDtypeStruct((BLK, HEAD_DEVS * WIDTH), jnp.bfloat16),
        in_specs=[SMEM] + [VMEM] * (2 + HEAD_DEVS),
        out_specs=VMEM,
        compiler_params=params(32),
    )(me, query_rows[0], fetched, *local)
    return mixed[None]


def solution(mesh):
    placed = (
        P("mem", "head", None),
        P("mem", "head", None),
        P("mem", "head", None),
        P("mem", None, "head"),
        P("mem", None, "head"),
        P("mem", None, None),
        P("mem", None, None),
        P("head"),
    )
    return jax.shard_map(
        on_device, mesh=mesh, in_specs=placed, out_specs=P("mem", "head", None), check_vma=False
    )
```

time: 607 us -> 191 us (0.31)
  the two profiles are of different devices: /device:TPU:102 before, /device:TPU:6 now
where the time goes in v1:
time: 191 us; the launch traced here: 187 us
  blocking collectives  65 us (34%)
  waiting for transfers between devices  53.4 us (28%)
  starting transfers between devices  45.6 us (24%)
  Pallas kernels  16.9 us (9%)
  local copies, waits for them, and re-layouts  4.81 us (3%)
    all_to_all x1, blocking collectives, on_device(): lax.all_to_all(spread, 'mem', split_axis=0, concat_axis=0, tiled=True)  65 us
    ppermute x14, waiting for transfers between devices, rotated(): lax.ppermute(arrays[s], 'head', [(i, (i + s) % HEAD_DEVS) for i in range(...  53.4 us
    ppermute x14, starting transfers between devices, rotated(): lax.ppermute(arrays[s], 'head', [(i, (i + s) % HEAD_DEVS) for i in range(...  36.2 us
    all_to_all x1, starting transfers between devices, on_device(): lax.all_to_all(requested, ('mem', 'head'), split_axis=0, concat_axis=0, t...  9.31 us
    pallas_call x1, Pallas kernels, on_device(): pl.pallas_call(local_kernel, out_shape=[jax.ShapeDtypeStruct((WIDTH + ROW...  7.03 us
    pallas_call x1, Pallas kernels, on_device(): pl.pallas_call(mix_kernel, out_shape=jax.ShapeDtypeStruct((BLK, HEAD_DEVS...  5.02 us
    unnamed x14, local copies, waits for them, and re-layouts  4.47 us
    pallas_call x1, Pallas kernels, on_device(): pl.pallas_call(gather_kernel, out_shape=jax.ShapeDtypeStruct((MEM_DEVS *...  4.27 us
  transfers between devices with their start and end apart: 15, of which 12 were waited for; matrix products, arithmetic and copies ran while one was open for 0% of the time, Pallas kernels for 4%

profile of v1, /device:TPU:6, one launch (start us, length us, event | category | flops | bytes accessed | tf_op | source)
XLA Modules:
  0.0 187.2 jit_solution(18263248291370579401)
XLA Ops:
  0.0 0.7 add_convert_fusion
  1.0 1.2 copy-done.2
  2.2 1.2 copy-done.3
  3.4 0.4 shard_map.82
  3.8 65.0 %all_to_all.10.table_ref = bf16[32,17,16,128]{3,2,1,0:T(8,128)(2,1)S(1)} all-to-all(bf16[32,17,16,128]{3,2,1,0:T(8,128)(2,1)S(1)} %shard_map.82), channel_id=1, replica_groups=mesh['mem'=32,'head'=8] {'mem'}, dimensions={0} | all-to-all | bytes 4456448 | tf_op jit(solution)/shard_map/all_to_all | solution.py:163
  68.8 0.6 convert_reduce_fusion
  69.5 4.3 %shard_map.83 = bf16[256,2,2,16,128]{4,3,2,1,0:T(8,128)(2,1)S(1)} custom-call(s32[512]{0:T(512)S(1)} %reshape.21.ids_ref, bf16[32,17,16,128]{3,2,1,0:T(8,128)(2,1)S(1)} %all_to_all.10.table_ref), custom_call_target="tpu_custom_call" | custom-call | tf_op jit(solution)/shard_map/pallas_call | solution.py:187
  73.8 2.0 %copy-done = bf16[256,2,2,16,128]{4,3,2,1,0:T(8,128)(2,1)} copy-done((bf16[256,2,2,16,128]{4,3,2,1,0:T(8,128)(2,1)}, bf16[256,2,2,16,128]{4,3,2,1,0:T(8,128)(2,1)S(1)}, u32[]{:S(2)}) %copy-start) | copy-done | bytes 4194328
  75.8 9.3 %all-to-all-start.1 = ((bf16[256,2,2,16,128]{4,3,2,1,0:T(8,128)(2,1)}), bf16[256,2,2,16,128]{4,3,2,1,0:T(8,128)(2,1)}, u32[]{:S(2)}, u32[]{:S(2)}) async-start(bf16[256,2,2,16,128]{4,3,2,1,0:T(8,128)(2,1)} %copy-done), calls=%async_computation.1 | async-start | bytes 8388608 | tf_op jit(solution)/shard_map/all_to_all | solution.py:194
  85.6 1.5 collective-permute-start.1
  87.1 2.0 %collective-permute-start.2 = (bf16[3,128,512]{2,1,0:T(8,128)(2,1)S(1)}, bf16[3,128,512]{2,1,0:T(8,128)(2,1)S(1)}, u32[]{:S(2)}, u32[]{:S(2)}) collective-permute-start(bf16[3,128,512]{2,1,0:T(8,128)(2,1)S(1)} %get-tuple-element.24), channel_id=1, source_target_pairs={{0,3},{1,4},{2,5},{3,6},{4,7},{5,0},{6,1},{7,2},{8,11},{9,12},{10,... | collective-permute-start | bytes 1179656 | tf_op jit(solution)/shard_map/ppermute | solution.py:148
  89.1 2.0 %collective-permute-start.3 = (bf16[3,128,512]{2,1,0:T(8,128)(2,1)S(1)}, bf16[3,128,512]{2,1,0:T(8,128)(2,1)S(1)}, u32[]{:S(2)}, u32[]{:S(2)}) collective-permute-start(bf16[3,128,512]{2,1,0:T(8,128)(2,1)S(1)} %get-tuple-element.25), channel_id=1, source_target_pairs={{0,4},{1,5},{2,6},{3,7},{4,0},{5,1},{6,2},{7,3},{8,12},{9,13},{10,... | collective-permute-start | bytes 1179656 | tf_op jit(solution)/shard_map/ppermute | solution.py:148
  91.0 1.8 collective-permute-start.4
  92.8 16.9 %collective-permute-done.refs_1_ = bf16[3,128,512]{2,1,0:T(8,128)(2,1)S(1)} collective-permute-done((bf16[3,128,512]{2,1,0:T(8,128)(2,1)S(1)}, bf16[3,128,512]{2,1,0:T(8,128)(2,1)S(1)}, u32[]{:S(2)}, u32[]{:S(2)}) %collective-permute-start) | collective-permute-done | bytes 393248 | tf_op jit(solution)/shard_map/ppermute | solution.py:148
  109.7 0.4 collective-permute-done.1.refs_2_
  110.1 14.9 %collective-permute-start.6 = (bf16[3,128,512]{2,1,0:T(8,128)(2,1)S(1)}, bf16[3,128,512]{2,1,0:T(8,128)(2,1)S(1)}, u32[]{:S(2)}, u32[]{:S(2)}) collective-permute-start(bf16[3,128,512]{2,1,0:T(8,128)(2,1)S(1)} %get-tuple-element.28), channel_id=1, source_target_pairs={{0,7},{1,0},{2,1},{3,2},{4,3},{5,4},{6,5},{7,6},{8,15},{9,8},{10,9... | collective-permute-start | bytes 1179656 | tf_op jit(solution)/shard_map/ppermute | solution.py:148
  125.0 14.1 %collective-permute-done.2.refs_3_ = bf16[3,128,512]{2,1,0:T(8,128)(2,1)S(1)} collective-permute-done((bf16[3,128,512]{2,1,0:T(8,128)(2,1)S(1)}, bf16[3,128,512]{2,1,0:T(8,128)(2,1)S(1)}, u32[]{:S(2)}, u32[]{:S(2)}) %collective-permute-start.2) | collective-permute-done | bytes 393248 | tf_op jit(solution)/shard_map/ppermute | solution.py:148
  139.1 12.1 %collective-permute-done.4.refs_5_ = bf16[3,128,512]{2,1,0:T(8,128)(2,1)S(1)} collective-permute-done((bf16[3,128,512]{2,1,0:T(8,128)(2,1)S(1)}, bf16[3,128,512]{2,1,0:T(8,128)(2,1)S(1)}, u32[]{:S(2)}, u32[]{:S(2)}) %collective-permute-start.4) | collective-permute-done | bytes 393248 | tf_op jit(solution)/shard_map/ppermute | solution.py:148
  151.3 0.4 collective-permute-done.6.refs_7_
  151.7 7.0 %shard_map.85 = (bf16[528,128]{1,0:T(8,128)(2,1)S(1)}, bf16[528,128]{1,0:T(8,128)(2,1)S(1)}, bf16[528,128]{1,0:T(8,128)(2,1)S(1)}, bf16[528,128]{1,0:T(8,128)(2,...) custom-call(s32[1]{0:T(128)} %bitcast.me_ref, ...), custom_call_target="tpu_custom_call" | custom-call | tf_op jit(solution)/shard_map/pallas_call | solution.py:173
  158.7 3.9 %collective-permute-start.7 = (bf16[528,128]{1,0:T(8,128)(2,1)S(1)}, bf16[528,128]{1,0:T(8,128)(2,1)S(1)}, u32[]{:S(2)}, u32[]{:S(2)}) collective-permute-start(bf16[528,128]{1,0:T(8,128)(2,1)S(1)} %get-tuple-element.30), channel_id=1, source_target_pairs={{0,1},{1,2},{2,3},{3,4},{4,5},{5,6},{6,7},{7,0},{8,9},{9,10},{10,1... | collective-permute-start | bytes 405512 | tf_op jit(solution)/shard_map/ppermute | solution.py:148
  162.6 0.7 collective-permute-start.9
  163.4 3.4 %collective-permute-start.10 = (bf16[528,128]{1,0:T(8,128)(2,1)S(1)}, bf16[528,128]{1,0:T(8,128)(2,1)S(1)}, u32[]{:S(2)}, u32[]{:S(2)}) collective-permute-start(bf16[528,128]{1,0:T(8,128)(2,1)S(1)} %get-tuple-element.33), channel_id=1, source_target_pairs={{0,4},{1,5},{2,6},{3,7},{4,0},{5,1},{6,2},{7,3},{8,12},{9,13},{10,... | collective-permute-start | bytes 405512 | tf_op jit(solution)/shard_map/ppermute | solution.py:148
  166.8 0.3 collective-permute-start.11
  167.1 2.5 %collective-permute-start.12 = (bf16[528,128]{1,0:T(8,128)(2,1)S(1)}, bf16[528,128]{1,0:T(8,128)(2,1)S(1)}, u32[]{:S(2)}, u32[]{:S(2)}) collective-permute-start(bf16[528,128]{1,0:T(8,128)(2,1)S(1)} %get-tuple-element.35), channel_id=1, source_target_pairs={{0,6},{1,7},{2,0},{3,1},{4,2},{5,3},{6,4},{7,5},{8,14},{9,15},{10,... | collective-permute-start | bytes 405512 | tf_op jit(solution)/shard_map/ppermute | solution.py:148
  169.6 0.8 collective-permute-done.8.refs_2_
  170.4 3.1 %collective-permute-start.13 = (bf16[528,128]{1,0:T(8,128)(2,1)S(1)}, bf16[528,128]{1,0:T(8,128)(2,1)S(1)}, u32[]{:S(2)}, u32[]{:S(2)}) collective-permute-start(bf16[528,128]{1,0:T(8,128)(2,1)S(1)} %get-tuple-element.36), channel_id=1, source_target_pairs={{0,7},{1,0},{2,1},{3,2},{4,3},{5,4},{6,5},{7,6},{8,15},{9,8},{10,9... | collective-permute-start | bytes 405512 | tf_op jit(solution)/shard_map/ppermute | solution.py:148
  173.5 5.8 %collective-permute-done.9.refs_3_ = bf16[528,128]{1,0:T(8,128)(2,1)S(1)} collective-permute-done((bf16[528,128]{1,0:T(8,128)(2,1)S(1)}, bf16[528,128]{1,0:T(8,128)(2,1)S(1)}, u32[]{:S(2)}, u32[]{:S(2)}) %collective-permute-start.9) | collective-permute-done | bytes 135200 | tf_op jit(solution)/shard_map/ppermute | solution.py:148
  179.4 1.3 collective-permute-done.10.refs_4_
  180.7 0.4 collective-permute-done.11.refs_5_
  181.2 1.0 collective-permute-done.13.refs_7_
  182.2 5.0 %shard_map.86 = bf16[128,4096]{1,0:T(8,128)(2,1)} custom-call(s32[1]{0:T(128)} %bitcast.me_ref, bf16[128,4096]{1,0:T(8,128)(2,1)S(1)} %bitcast.7, bf16[8,4,8,2,2,16,128]{6,5,4,3,2,1,0:T(8,128)(2,1)} %bitcast.2.fetched_ref, bf16[528,128]{1,0:T(8,128)(2,1)S(1)} %get-tuple-element.29.refs_0_, bf16[528,128]{1,0:T(8,128)(2,1)S(1)} %collective-permute-done.7.refs_1_, ...), custom_call_target="tpu_custom_call" | custom-call | tf_op jit(solution)/shard_map/pallas_call | solution.py:196
  (24 shorter events, 1.0 us)
Async XLA Ops:
  1.0 1.2 copy-start.2
  2.2 1.2 copy-start.3
  73.8 2.0 %copy-start = (bf16[256,2,2,16,128]{4,3,2,1,0:T(8,128)(2,1)}, bf16[256,2,2,16,128]{4,3,2,1,0:T(8,128)(2,1)S(1)}, u32[]{:S(2)}) copy-start(bf16[256,2,2,16,128]{4,3,2,1,0:T(8,128)(2,1)S(1)} %shard_map.83) | copy-start | bytes 12582916
  75.8 9.3 %copy-start.1 = (bf16[1,128,4096]{2,1,0:T(8,128)(2,1)S(1)}, bf16[1,128,4096]{2,1,0:T(8,128)(2,1)}, u32[]{:S(2)}) copy-start(bf16[1,128,4096]{2,1,0:T(8,128)(2,1)} %param.8) | copy-start | bytes 3145732
  75.8 9.4 %copy-start.4 = (bf16[1,128,4096]{2,1,0:T(8,128)(2,1)S(1)}, bf16[1,128,4096]{2,1,0:T(8,128)(2,1)}, u32[]{:S(2)}) copy-start(bf16[1,128,4096]{2,1,0:T(8,128)(2,1)} %param.9) | copy-start | bytes 3145732
  75.8 9.4 %copy-start.5 = (bf16[1,128,4096]{2,1,0:T(8,128)(2,1)S(1)}, bf16[1,128,4096]{2,1,0:T(8,128)(2,1)}, u32[]{:S(2)}) copy-start(bf16[1,128,4096]{2,1,0:T(8,128)(2,1)} %param.10) | copy-start | bytes 3145732
  75.8 106.4 %all-to-all-start.1 = ((bf16[256,2,2,16,128]{4,3,2,1,0:T(8,128)(2,1)}), bf16[256,2,2,16,128]{4,3,2,1,0:T(8,128)(2,1)}, u32[]{:S(2)}, u32[]{:S(2)}) async-start(bf16[256,2,2,16,128]{4,3,2,1,0:T(8,128)(2,1)} %copy-done), calls=%async_computation.1 | async-start | bytes 8388608 | tf_op jit(solution)/shard_map/all_to_all | solution.py:194
  85.1 66.6 %copy-start.6 = (f32[4]{0:T(128)S(1)}, f32[4]{0:T(128)}, u32[]{:S(2)}) copy-start(f32[4]{0:T(128)} %gate_ref.1) | copy-start | bytes 52
  85.4 24.2 %collective-permute-start = (bf16[3,128,512]{2,1,0:T(8,128)(2,1)S(1)}, bf16[3,128,512]{2,1,0:T(8,128)(2,1)S(1)}, u32[]{:S(2)}, u32[]{:S(2)}) collective-permute-start(bf16[3,128,512]{2,1,0:T(8,128)(2,1)S(1)} %get-tuple-element.22), channel_id=1, source_target_pairs={{0,1},{1,2},{2,3},{3,4},{4,5},{5,6},{6,7},{7,0},{8,9},{9,10},{10,1... | collective-permute-start | bytes 1179656 | tf_op jit(solution)/shard_map/ppermute | solution.py:148
  85.6 24.5 %collective-permute-start.1 = (bf16[3,128,512]{2,1,0:T(8,128)(2,1)S(1)}, bf16[3,128,512]{2,1,0:T(8,128)(2,1)S(1)}, u32[]{:S(2)}, u32[]{:S(2)}) collective-permute-start(bf16[3,128,512]{2,1,0:T(8,128)(2,1)S(1)} %get-tuple-element.23), channel_id=1, source_target_pairs={{0,2},{1,3},{2,4},{3,5},{4,6},{5,7},{6,0},{7,1},{8,10},{9,11},{10,... | collective-permute-start | bytes 1179656 | tf_op jit(solution)/shard_map/ppermute | solution.py:148
  87.1 52.0 %collective-permute-start.2 = (bf16[3,128,512]{2,1,0:T(8,128)(2,1)S(1)}, bf16[3,128,512]{2,1,0:T(8,128)(2,1)S(1)}, u32[]{:S(2)}, u32[]{:S(2)}) collective-permute-start(bf16[3,128,512]{2,1,0:T(8,128)(2,1)S(1)} %get-tuple-element.24), channel_id=1, source_target_pairs={{0,3},{1,4},{2,5},{3,6},{4,7},{5,0},{6,1},{7,2},{8,11},{9,12},{10,... | collective-permute-start | bytes 1179656 | tf_op jit(solution)/shard_map/ppermute | solution.py:148
  89.1 50.0 %collective-permute-start.3 = (bf16[3,128,512]{2,1,0:T(8,128)(2,1)S(1)}, bf16[3,128,512]{2,1,0:T(8,128)(2,1)S(1)}, u32[]{:S(2)}, u32[]{:S(2)}) collective-permute-start(bf16[3,128,512]{2,1,0:T(8,128)(2,1)S(1)} %get-tuple-element.25), channel_id=1, source_target_pairs={{0,4},{1,5},{2,6},{3,7},{4,0},{5,1},{6,2},{7,3},{8,12},{9,13},{10,... | collective-permute-start | bytes 1179656 | tf_op jit(solution)/shard_map/ppermute | solution.py:148
  91.0 60.2 %collective-permute-start.4 = (bf16[3,128,512]{2,1,0:T(8,128)(2,1)S(1)}, bf16[3,128,512]{2,1,0:T(8,128)(2,1)S(1)}, u32[]{:S(2)}, u32[]{:S(2)}) collective-permute-start(bf16[3,128,512]{2,1,0:T(8,128)(2,1)S(1)} %get-tuple-element.26), channel_id=1, source_target_pairs={{0,5},{1,6},{2,7},{3,0},{4,1},{5,2},{6,3},{7,4},{8,13},{9,14},{10,... | collective-permute-start | bytes 1179656 | tf_op jit(solution)/shard_map/ppermute | solution.py:148
  109.7 41.6 %collective-permute-start.5 = (bf16[3,128,512]{2,1,0:T(8,128)(2,1)S(1)}, bf16[3,128,512]{2,1,0:T(8,128)(2,1)S(1)}, u32[]{:S(2)}, u32[]{:S(2)}) collective-permute-start(bf16[3,128,512]{2,1,0:T(8,128)(2,1)S(1)} %get-tuple-element.27), channel_id=1, source_target_pairs={{0,6},{1,7},{2,0},{3,1},{4,2},{5,3},{6,4},{7,5},{8,14},{9,15},{10,... | collective-permute-start | bytes 1179656 | tf_op jit(solution)/shard_map/ppermute | solution.py:148
  110.1 41.6 %collective-permute-start.6 = (bf16[3,128,512]{2,1,0:T(8,128)(2,1)S(1)}, bf16[3,128,512]{2,1,0:T(8,128)(2,1)S(1)}, u32[]{:S(2)}, u32[]{:S(2)}) collective-permute-start(bf16[3,128,512]{2,1,0:T(8,128)(2,1)S(1)} %get-tuple-element.28), channel_id=1, source_target_pairs={{0,7},{1,0},{2,1},{3,2},{4,3},{5,4},{6,5},{7,6},{8,15},{9,8},{10,9... | collective-permute-start | bytes 1179656 | tf_op jit(solution)/shard_map/ppermute | solution.py:148
  158.7 8.3 %collective-permute-start.7 = (bf16[528,128]{1,0:T(8,128)(2,1)S(1)}, bf16[528,128]{1,0:T(8,128)(2,1)S(1)}, u32[]{:S(2)}, u32[]{:S(2)}) collective-permute-start(bf16[528,128]{1,0:T(8,128)(2,1)S(1)} %get-tuple-element.30), channel_id=1, source_target_pairs={{0,1},{1,2},{2,3},{3,4},{4,5},{5,6},{6,7},{7,0},{8,9},{9,10},{10,1... | collective-permute-start | bytes 405512 | tf_op jit(solution)/shard_map/ppermute | solution.py:148
  162.6 7.8 %collective-permute-start.8 = (bf16[528,128]{1,0:T(8,128)(2,1)S(1)}, bf16[528,128]{1,0:T(8,128)(2,1)S(1)}, u32[]{:S(2)}, u32[]{:S(2)}) collective-permute-start(bf16[528,128]{1,0:T(8,128)(2,1)S(1)} %get-tuple-element.31), channel_id=1, source_target_pairs={{0,2},{1,3},{2,4},{3,5},{4,6},{5,7},{6,0},{7,1},{8,10},{9,11},{10,... | collective-permute-start | bytes 405512 | tf_op jit(solution)/shard_map/ppermute | solution.py:148
  162.6 16.7 %collective-permute-start.9 = (bf16[528,128]{1,0:T(8,128)(2,1)S(1)}, bf16[528,128]{1,0:T(8,128)(2,1)S(1)}, u32[]{:S(2)}, u32[]{:S(2)}) collective-permute-start(bf16[528,128]{1,0:T(8,128)(2,1)S(1)} %get-tuple-element.32), channel_id=1, source_target_pairs={{0,3},{1,4},{2,5},{3,6},{4,7},{5,0},{6,1},{7,2},{8,11},{9,12},{10,... | collective-permute-start | bytes 405512 | tf_op jit(solution)/shard_map/ppermute | solution.py:148
  163.4 17.3 %collective-permute-start.10 = (bf16[528,128]{1,0:T(8,128)(2,1)S(1)}, bf16[528,128]{1,0:T(8,128)(2,1)S(1)}, u32[]{:S(2)}, u32[]{:S(2)}) collective-permute-start(bf16[528,128]{1,0:T(8,128)(2,1)S(1)} %get-tuple-element.33), channel_id=1, source_target_pairs={{0,4},{1,5},{2,6},{3,7},{4,0},{5,1},{6,2},{7,3},{8,12},{9,13},{10,... | collective-permute-start | bytes 405512 | tf_op jit(solution)/shard_map/ppermute | solution.py:148
  166.8 14.3 %collective-permute-start.11 = (bf16[528,128]{1,0:T(8,128)(2,1)S(1)}, bf16[528,128]{1,0:T(8,128)(2,1)S(1)}, u32[]{:S(2)}, u32[]{:S(2)}) collective-permute-start(bf16[528,128]{1,0:T(8,128)(2,1)S(1)} %get-tuple-element.34), channel_id=1, source_target_pairs={{0,5},{1,6},{2,7},{3,0},{4,1},{5,2},{6,3},{7,4},{8,13},{9,14},{10,... | collective-permute-start | bytes 405512 | tf_op jit(solution)/shard_map/ppermute | solution.py:148
  167.1 14.1 %collective-permute-start.12 = (bf16[528,128]{1,0:T(8,128)(2,1)S(1)}, bf16[528,128]{1,0:T(8,128)(2,1)S(1)}, u32[]{:S(2)}, u32[]{:S(2)}) collective-permute-start(bf16[528,128]{1,0:T(8,128)(2,1)S(1)} %get-tuple-element.35), channel_id=1, source_target_pairs={{0,6},{1,7},{2,0},{3,1},{4,2},{5,3},{6,4},{7,5},{8,14},{9,15},{10,... | collective-permute-start | bytes 405512 | tf_op jit(solution)/shard_map/ppermute | solution.py:148
  170.4 11.7 %collective-permute-start.13 = (bf16[528,128]{1,0:T(8,128)(2,1)S(1)}, bf16[528,128]{1,0:T(8,128)(2,1)S(1)}, u32[]{:S(2)}, u32[]{:S(2)}) collective-permute-start(bf16[528,128]{1,0:T(8,128)(2,1)S(1)} %get-tuple-element.36), channel_id=1, source_target_pairs={{0,7},{1,0},{2,1},{3,2},{4,3},{5,4},{6,5},{7,6},{8,15},{9,8},{10,9... | collective-permute-start | bytes 405512 | tf_op jit(solution)/shard_map/ppermute | solution.py:148

commit v2 on v1

v2 whole, which is shorter than its diff:
```python
import functools
import math

import jax
import jax.numpy as jnp
from jax import lax
from jax.experimental import pallas as pl
from jax.experimental.pallas import tpu as pltpu
from jax.sharding import Mesh
from jax.sharding import PartitionSpec as P

DH = 128
BLK = 128
HEADS_DEV = 4
CHIPS = 4
CORES = 2
HEAD_DEVS = CHIPS * CORES
PLANES = 8
MEM_DEVS = 32
PLANE_DEVS = 32
SLOTS = 8
ROWS = 32
TAIL = 16
FAR = (4, 3, 5, 2, 6)
NEAR = (0, 1, 7)
WIDTH = HEADS_DEV * DH
Q_TILE = 256
EXP_SCALE = math.log2(math.e) / math.sqrt(DH)
MASKED = -1e30


def whole(array):
    ndim = len(array.shape)
    return pl.BlockSpec(array.shape, lambda i: (0,) * ndim, pipeline_mode=pl.Buffered(1))


def call(kernel, outs, scalars, arrays, scratch=(), mib=12, hbm=()):
    outs = [pltpu.HBM(shape, jnp.bfloat16) for shape in outs]
    return pl.pallas_call(
        kernel,
        out_shape=outs,
        grid=(1,),
        in_specs=[pl.BlockSpec(memory_space=pltpu.SMEM)] * len(scalars) + [whole(a) for a in arrays],
        out_specs=[whole(o) for o in outs],
        scratch_shapes=[pltpu.VMEM(shape, jnp.bfloat16) for shape in scratch],
        compiler_params=pltpu.CompilerParams(vmem_limit_bytes=mib * 1024 * 1024),
    )(
        *scalars,
        *[
            pltpu.with_memory_space_constraint(a, pltpu.HBM) if i in hbm else a
            for i, a in enumerate(arrays)
        ],
    )


def dot_nt(a, b):
    return lax.dot_general(a, b, (((1,), (1,)), ((), ())), preferred_element_type=jnp.float32)


def spread_kernel(core_ref, keys_ref, values_ref, swapped_ref, ids_ref, out_ref):
    core = core_ref[0]
    for j in range(HEADS_DEV):
        for x in range(BLK // ROWS):
            rows, cols = pl.ds(x * ROWS, ROWS), pl.ds(j * DH, DH)
            kept = jnp.where(core == 0, keys_ref[:, rows, cols], values_ref[:, rows, cols])
            for source, piece in ((core, kept), (1 - core, swapped_ref[:, rows, cols])):
                dest = (source * HEADS_DEV + j) * (BLK // ROWS) + x
                out_ref[dest, pl.ds(0, SLOTS * ROWS), :] = piece.reshape(SLOTS * ROWS, DH)
    for dest in range(MEM_DEVS):
        out_ref[dest, pl.ds(SLOTS * ROWS, TAIL), :] = ids_ref[...]


def gather_kernel(shifts, z_ref, ids_ref, table_ref, out_ref):
    def one(dest, carry):
        for i, shift in enumerate(shifts):
            plane = (z_ref[0] + PLANES - shift) & (PLANES - 1)
            for k in range(2):
                block = ids_ref[plane * 2 * PLANE_DEVS + 2 * dest + k]
                first = pl.multiple_of((block & (SLOTS - 1)) * ROWS, ROWS)
                owner = lax.shift_right_logical(block, 3)
                out_ref[dest, 2 * i + k] = table_ref[owner, pl.ds(first, ROWS), :]
        return carry

    lax.fori_loop(0, PLANE_DEVS, one, 0, unroll=4)


def query_kernel(z_ref, q_ref, *out_refs):
    for shift in range(PLANES):
        plane = (z_ref[0] + shift) % PLANES
        for y in range(HEADS_DEV):
            cols = pl.ds(pl.multiple_of((y * PLANES + plane) * DH, DH), DH)
            out_refs[shift][y] = q_ref[:, cols]


def attend_kernel(count, *refs):
    queries, fetched_ref, outs = refs[:count], refs[count], refs[count + 1 :]
    for i in range(count):
        for y in range(HEADS_DEV):
            keys = fetched_ref[:, y, 0, pl.ds(2 * i, 2)].reshape(2 * BLK, DH)
            values = fetched_ref[:, y, 1, pl.ds(2 * i, 2)].reshape(2 * BLK, DH)
            scores = dot_nt(queries[i][y], keys)
            top = jnp.max(scores, axis=1, keepdims=True)
            weights = jnp.exp2((scores - top) * EXP_SCALE)
            total = jnp.sum(weights, axis=1, keepdims=True)
            part = jnp.dot(weights.astype(jnp.bfloat16), values, preferred_element_type=jnp.float32)
            outs[i][y] = (part / total).astype(jnp.bfloat16)


def pack_kernel(me_ref, q_ref, k_ref, v_ref, *out_refs):
    for shift in range(HEAD_DEVS):
        dest = (me_ref[0] + shift) % HEAD_DEVS
        cols = pl.ds(pl.multiple_of(dest * WIDTH, WIDTH), WIDTH)
        for i, ref in enumerate((q_ref, k_ref, v_ref)):
            out_refs[shift][i] = ref[:, cols]


def local_kernel(me_ref, gate_ref, *refs):
    ins, outs = refs[:HEAD_DEVS], refs[HEAD_DEVS : HEAD_DEVS + CORES]
    held, result = refs[HEAD_DEVS + CORES :]
    me = me_ref[0]
    for shift in range(HEAD_DEVS):
        held[:, (me + HEAD_DEVS - shift) % HEAD_DEVS] = ins[shift][...]
    length = HEAD_DEVS * BLK
    blocks = Q_TILE // BLK
    parts = []
    for j in range(HEADS_DEV):
        cols = pl.ds(j * DH, DH)
        gate = jax.nn.sigmoid(jnp.full((1, DH), gate_ref[j], jnp.float32))
        high = gate.astype(jnp.bfloat16)
        rest = gate - high.astype(jnp.float32)
        mid = rest.astype(jnp.bfloat16)
        low = (rest - mid.astype(jnp.float32)).astype(jnp.bfloat16)
        parts.append((high, mid, low))
        for tile in range(length // Q_TILE):
            rows = pl.ds(tile * blocks, blocks)
            query = held[0, rows, :, cols].reshape(Q_TILE, DH)
            diag = dot_nt(query, held[1, rows, :, cols].reshape(Q_TILE, DH))
            row_ids = lax.broadcasted_iota(jnp.int32, (Q_TILE, Q_TILE), 0)
            col_ids = lax.broadcasted_iota(jnp.int32, (Q_TILE, Q_TILE), 1)
            diag = jnp.where(col_ids <= row_ids, diag, MASKED)
            top = jnp.max(diag, axis=1, keepdims=True)
            if tile:
                before = pl.ds(0, tile * blocks)
                off = dot_nt(query, held[1, before, :, cols].reshape(tile * Q_TILE, DH))
                top = jnp.maximum(top, jnp.max(off, axis=1, keepdims=True))
            weights = jnp.exp2((diag - top) * EXP_SCALE)
            total = jnp.sum(weights, axis=1, keepdims=True)
            part = jnp.dot(
                weights.astype(jnp.bfloat16),
                held[2, rows, :, cols].reshape(Q_TILE, DH),
                preferred_element_type=jnp.float32,
            )
            if tile:
                weights = jnp.exp2((off - top) * EXP_SCALE)
                total = total + jnp.sum(weights, axis=1, keepdims=True)
                part = part + jnp.dot(
                    weights.astype(jnp.bfloat16),
                    held[2, before, :, cols].reshape(tile * Q_TILE, DH),
                    preferred_element_type=jnp.float32,
                )
            part = part * ((1.0 - gate) / total)
            result[rows, j] = part.astype(jnp.bfloat16).reshape(blocks, BLK, DH)
    for i, out in enumerate(outs):
        for chip in range(CHIPS):
            out[chip, :, pl.ds(0, BLK), :] = result[chip * CORES + (me + i) % CORES]
            for j in range(HEADS_DEV):
                filler = jnp.zeros((TAIL - 3, DH), jnp.bfloat16)
                rows = jnp.concatenate([*parts[j], filler], axis=0)
                out[chip, j, pl.ds(BLK, TAIL), :] = rows


def merge_kernel(me_ref, own_ref, other_ref, *out_refs):
    core = me_ref[0] % CORES
    for shift in range(CHIPS):
        chip = (me_ref[0] // CORES + shift) % CHIPS
        out_refs[shift][core] = own_ref[chip]
        out_refs[shift][1 - core] = other_ref[chip]


def mix_kernel(me_ref, z_ref, *refs):
    memory, local = refs[:PLANES], refs[PLANES : PLANES + CHIPS]
    out_ref, held = refs[PLANES + CHIPS :]
    for shift in range(CHIPS):
        chip = (me_ref[0] // CORES + CHIPS - shift) % CHIPS
        for core in range(CORES):
            first = (chip * CORES + core) * HEADS_DEV
            held[pl.ds(first, HEADS_DEV)] = local[shift][core]
    for shift in range(PLANES):
        plane = (z_ref[0] + shift) % PLANES
        for y in range(HEADS_DEV):
            head = y * PLANES + plane
            gate = held[head, pl.ds(BLK, TAIL), :].astype(jnp.float32)
            gate = gate[0:1] + gate[1:2] + gate[2:3]
            part = memory[shift][y].astype(jnp.float32) * gate
            part = part + held[head, pl.ds(0, BLK), :].astype(jnp.float32)
            out_ref[:, pl.ds(pl.multiple_of(head * DH, DH), DH)] = part.astype(jnp.bfloat16)


def shifted(array, axis, size, shift):
    if shift % size == 0:
        return array
    return lax.ppermute(array, axis, [(i, (i + shift) % size) for i in range(size)])


def on_device(
    query_rows, key_rows, value_rows, memory_keys, memory_values, owner_list, slot_list, gate_logit
):
    core = lax.axis_index("c")
    z = lax.axis_index("z").astype(jnp.int32).reshape(1)
    me = lax.axis_index(("y", "c")).astype(jnp.int32).reshape(1)
    query = query_rows[0]

    swapped = shifted(jnp.where(core == 0, memory_values, memory_keys), "c", CORES, 1)
    ids = (owner_list * SLOTS + slot_list).reshape(TAIL, 1)
    ids = jnp.broadcast_to(ids.astype(jnp.bfloat16), (TAIL, DH))
    (spread,) = call(
        spread_kernel,
        [(MEM_DEVS, SLOTS * ROWS + TAIL, DH)],
        [core.astype(jnp.int32).reshape(1)],
        [memory_keys, memory_values, swapped, ids],
    )
    table = lax.all_to_all(spread, ("z", "x"), split_axis=0, concat_axis=0, tiled=True)

    packed = call(
        pack_kernel, [(3, BLK, WIDTH)] * HEAD_DEVS, [me], [query, key_rows[0], value_rows[0]]
    )
    packed = [shifted(packed[s], ("y", "c"), HEAD_DEVS, s) for s in range(HEAD_DEVS)]
    local = call(
        local_kernel,
        [(CHIPS, HEADS_DEV, BLK + TAIL, DH)] * CORES,
        [me, gate_logit],
        packed,
        [(3, HEAD_DEVS, BLK, WIDTH), (HEAD_DEVS, HEADS_DEV, BLK, DH)],
        24,
        range(HEAD_DEVS),
    )
    table, local = lax.optimization_barrier((table, local))

    all_ids = table[:, SLOTS * ROWS :, 0].astype(jnp.int32).reshape(MEM_DEVS * TAIL)

    def gathered(shifts, table):
        return call(
            functools.partial(gather_kernel, shifts),
            [(PLANE_DEVS, 2 * len(shifts), ROWS, DH)],
            [z, all_ids],
            [table],
        )[0]

    def fetch(requested):
        fetched = lax.all_to_all(
            requested, ("x", "y", "c"), split_axis=0, concat_axis=0, tiled=True
        )
        return fetched.reshape(BLK // ROWS, HEADS_DEV, 2, -1, ROWS, DH)

    def attend(shifts, fetched):
        return call(
            functools.partial(attend_kernel, len(shifts)),
            [(HEADS_DEV, BLK, DH)] * len(shifts),
            [],
            [asked[s] for s in shifts] + [fetched],
            hbm=range(len(shifts)),
        )

    far, table, query, local = lax.optimization_barrier((gathered(FAR, table), table, query, local))
    far = fetch(far)
    near = gathered(NEAR, table)
    local = [local[0], shifted(local[1], "c", CORES, 1)]
    local = call(merge_kernel, [(CORES, HEADS_DEV, BLK + TAIL, DH)] * CHIPS, [me], local)
    asked = call(query_kernel, [(HEADS_DEV, BLK, DH)] * PLANES, [z], [query])
    asked = [shifted(asked[s], "z", PLANES, s) for s in range(PLANES)]
    far, near, asked, local = lax.optimization_barrier((far, near, asked, local))

    near = fetch(near)
    memory = {s: shifted(part, "z", PLANES, -s) for s, part in zip(FAR, attend(FAR, far))}
    memory[6], local = lax.optimization_barrier((memory[6], local))
    local = [shifted(local[s], "y", CHIPS, s) for s in range(CHIPS)]
    memory.update({s: shifted(part, "z", PLANES, -s) for s, part in zip(NEAR, attend(NEAR, near))})

    (mixed,) = call(
        mix_kernel,
        [(BLK, HEAD_DEVS * WIDTH)],
        [me, z],
        [memory[s] for s in range(PLANES)] + local,
        [(HEAD_DEVS * HEADS_DEV, BLK + TAIL, DH)],
        hbm=range(PLANES + CHIPS),
    )
    return mixed[None]


def solution(mesh):
    fine = Mesh(mesh.devices.reshape(8, 4, 4, 2), ("z", "x", "y", "c"))
    mem, head = ("z", "x"), ("y", "c")
    placed = (
        P(mem, head, None),
        P(mem, head, None),
        P(mem, head, None),
        P(mem, None, head),
        P(mem, None, head),
        P(mem, None, None),
        P(mem, None, None),
        P(head),
    )
    return jax.shard_map(
        on_device, mesh=fine, in_specs=placed, out_specs=P(mem, head, None), check_vma=False
    )
```

time: 191 us -> 174 us (0.911)
  blocking collectives: 65 us -> 0 us
  starting transfers between devices: 45.6 us -> 94.5 us
  Pallas kernels: 16.9 us -> 30.8 us
  waiting for transfers between devices: 53.4 us -> 39.6 us
    all_to_all x1 -> x0, blocking collectives: 65 us -> none  [on_device(): lax.all_to_all(spread, 'mem', split_axis=0, concat_axis=0, tiled=True)]
    ppermute x14 -> x26, starting transfers between devices: 36.2 us -> 67.4 us  [shifted(): lax.ppermute(array, axis, [(i, (i + shift) % size) for i in range(size)])]
    all_to_all x1 -> x3, starting transfers between devices: 9.31 us -> 27.1 us  [the longest x2 15.4 us: fetch(): lax.all_to_all(requested, ('x', 'y', 'c'), split_axis=0, concat_axis=0, t...]
    ppermute x14 -> x26, waiting for transfers between devices: 53.4 us -> 39.4 us  [shifted(): lax.ppermute(array, axis, [(i, (i + shift) % size) for i in range(size)])]
    pallas_call x5 -> x10, Pallas kernels: 16.9 us -> 30.8 us  [call(): pl.pallas_call(kernel, out_shape=outs, grid=(1,), in_specs=[pl.BlockSpec(...]
    select_n x0 -> x1, other arithmetic: none -> 2.46 us  [on_device(): jnp.where(core == 0, memory_values, memory_keys)]
    unnamed x14 -> x52, local copies, waits for them, and re-layouts: 4.47 us -> 3.11 us
  transfers between devices with their start and end apart: 15 -> 29, of which waited for: 12 -> 15; matrix products, arithmetic and copies ran while one was open for 0% -> 0% of each run, Pallas kernels for 4% -> 13%
where the time goes in v2:
time: 174 us; the launch traced here: 172 us
  starting transfers between devices  94.5 us (54%)
  waiting for transfers between devices  39.6 us (23%)
  Pallas kernels  30.8 us (18%)
  local copies, waits for them, and re-layouts  3.44 us (2%)
  other arithmetic  3.08 us (2%)
    ppermute x26, starting transfers between devices, shifted(): lax.ppermute(array, axis, [(i, (i + shift) % size) for i in range(size)])  67.4 us
    ppermute x26, waiting for transfers between devices, shifted(): lax.ppermute(array, axis, [(i, (i + shift) % size) for i in range(size)])  39.4 us
    pallas_call x10, Pallas kernels, call(): pl.pallas_call(kernel, out_shape=outs, grid=(1,), in_specs=[pl.BlockSpec(...  30.8 us
    all_to_all x2, starting transfers between devices, fetch(): lax.all_to_all(requested, ('x', 'y', 'c'), split_axis=0, concat_axis=0, t...  15.4 us
    all_to_all x1, starting transfers between devices, on_device(): lax.all_to_all(spread, ('z', 'x'), split_axis=0, concat_axis=0, tiled=True)  11.7 us
  transfers between devices with their start and end apart: 29, of which 15 were waited for; matrix products, arithmetic and copies ran while one was open for 0% of the time, Pallas kernels for 13%

profile of v2, /device:TPU:6, one launch (start us, length us, event | category | flops | bytes accessed | tf_op | source)
XLA Modules:
  0.0 171.8 jit_solution(15063890533951564261)
XLA Ops:
  0.0 2.5 %broadcast_select_fusion = bf16[8,128,512]{2,1,0:T(8,128)(2,1)} fusion(bf16[8,128,512]{2,1,0:T(8,128)(2,1)} %values_ref.1, bf16[8,128,512]{2,1,0:T(8,128)(2,1)} %keys_ref.1, pred[]{:T(512)S(6)} %eq.3), kind=kLoop, calls=%fused_computation | loop fusion | flops 524288 | bytes 3145729 | tf_op jit(solution)/shard_map/jit(_where)/select_n | solution.py:213
  2.7 2.7 %collective-permute-done.swapped_ref = bf16[8,128,512]{2,1,0:T(8,128)(2,1)S(1)} collective-permute-done((bf16[8,128,512]{2,1,0:T(8,128)(2,1)}, bf16[8,128,512]{2,1,0:T(8,128)(2,1)S(1)}, u32[]{:S(2)}, u32[]{:S(2)}) %collective-permute-start) | collective-permute-done | bytes 1048608 | tf_op jit(solution)/shard_map/ppermute | solution.py:202
  7.3 11.7 %all-to-all-start = ((bf16[32,272,128]{2,1,0:T(8,128)(2,1)}), bf16[32,272,128]{2,1,0:T(8,128)(2,1)S(1)}, u32[]{:S(2)}, u32[]{:S(2)}) async-start(bf16[32,272,128]{2,1,0:T(8,128)(2,1)} %shard_map.82), calls=%async_computation | async-start | bytes 4456448 | tf_op jit(solution)/shard_map/all_to_all | solution.py:222
  25.0 2.3 %collective-permute-start.3 = (bf16[3,128,512]{2,1,0:T(8,128)(2,1)}, bf16[3,128,512]{2,1,0:T(8,128)(2,1)}, u32[]{:S(2)}, u32[]{:S(2)}) collective-permute-start(bf16[3,128,512]{2,1,0:T(8,128)(2,1)} %get-tuple-element.65), channel_id=1, source_target_pairs={{0,3},{1,4},{2,5},{3,6},{4,7},{5,0},{6,1},{7,2},{8,11},{9,12},{10,... | collective-permute-start | bytes 1179656 | tf_op jit(solution)/shard_map/ppermute | solution.py:202
  30.8 4.9 %collective-permute-done.1.refs_1_ = bf16[3,128,512]{2,1,0:T(8,128)(2,1)} collective-permute-done((bf16[3,128,512]{2,1,0:T(8,128)(2,1)}, bf16[3,128,512]{2,1,0:T(8,128)(2,1)}, u32[]{:S(2)}, u32[]{:S(2)}) %collective-permute-start.1) | collective-permute-done | bytes 393248 | tf_op jit(solution)/shard_map/ppermute | solution.py:202
  37.6 8.1 %collective-permute-start.7 = (bf16[3,128,512]{2,1,0:T(8,128)(2,1)}, bf16[3,128,512]{2,1,0:T(8,128)(2,1)}, u32[]{:S(2)}, u32[]{:S(2)}) collective-permute-start(bf16[3,128,512]{2,1,0:T(8,128)(2,1)} %get-tuple-element.69), channel_id=1, source_target_pairs={{0,7},{1,0},{2,1},{3,2},{4,3},{5,4},{6,5},{7,6},{8,15},{9,8},{10,9... | collective-permute-start | bytes 1179656 | tf_op jit(solution)/shard_map/ppermute | solution.py:202
  45.7 8.1 %collective-permute-done.3.refs_3_ = bf16[3,128,512]{2,1,0:T(8,128)(2,1)} collective-permute-done((bf16[3,128,512]{2,1,0:T(8,128)(2,1)}, bf16[3,128,512]{2,1,0:T(8,128)(2,1)}, u32[]{:S(2)}, u32[]{:S(2)}) %collective-permute-start.3) | collective-permute-done | bytes 393248 | tf_op jit(solution)/shard_map/ppermute | solution.py:202
  54.9 4.6 %collective-permute-done.5.refs_5_ = bf16[3,128,512]{2,1,0:T(8,128)(2,1)} collective-permute-done((bf16[3,128,512]{2,1,0:T(8,128)(2,1)}, bf16[3,128,512]{2,1,0:T(8,128)(2,1)}, u32[]{:S(2)}, u32[]{:S(2)}) %collective-permute-start.5) | collective-permute-done | bytes 393248 | tf_op jit(solution)/shard_map/ppermute | solution.py:202
  61.5 9.4 %shard_map.84 = (bf16[4,4,144,128]{3,2,1,0:T(8,128)(2,1)}, bf16[4,4,144,128]{3,2,1,0:T(8,128)(2,1)}) custom-call(s32[1]{0:T(128)} %bitcast.me_ref, f32[4]{0:T(128)S(1)} %copy-done.6, bf16[3,128,512]{2,1,0:T(8,128)(2,1)} %get-tuple-element.62.refs_0_, bf16[3,128,512]{2,1,0:T(8,128)(2,1)} %collective-permute-done.1.refs_1_, ...), custom_call_target="tpu_custom_call" | custom-call | tf_op jit(solution)/shard_map/pallas_call | solution.py:39
  71.9 3.1 %shard_map.85 = bf16[32,10,32,128]{3,2,1,0:T(8,128)(2,1)} custom-call(s32[1]{0:T(128)} %bitcast.1.z_ref, s32[512]{0:T(512)S(1)} %reshape.33.ids_ref, bf16[32,272,128]{2,1,0:T(8,128)(2,1)S(1)} %all-to-all-done.table_ref), custom_call_target="tpu_custom_call" | custom-call | tf_op jit(solution)/shard_map/pallas_call | solution.py:39
  75.0 8.1 %all-to-all-start.1 = ((bf16[32,10,32,128]{3,2,1,0:T(8,128)(2,1)}), bf16[32,10,32,128]{3,2,1,0:T(8,128)(2,1)}, u32[]{:S(2)}, u32[]{:S(2)}) async-start(bf16[32,10,32,128]{3,2,1,0:T(8,128)(2,1)} %shard_map.85), calls=%async_computation.1 | async-start | bytes 5242880 | tf_op jit(solution)/shard_map/all_to_all | solution.py:250
  86.3 2.2 %collective-permute-start.9 = (bf16[4,128,128]{2,1,0:T(8,128)(2,1)}, bf16[4,128,128]{2,1,0:T(8,128)(2,1)S(1)}, u32[]{:S(2)}, u32[]{:S(2)}) collective-permute-start(bf16[4,128,128]{2,1,0:T(8,128)(2,1)} %get-tuple-element.80), channel_id=1, source_target_pairs={{0,64},{32,96},{64,128},{96,160},{128,192},{160,224},{192,0},{224,... | collective-permute-start | bytes 393224 | tf_op jit(solution)/shard_map/ppermute | solution.py:202
  88.5 2.7 %collective-permute-start.10 = (bf16[4,128,128]{2,1,0:T(8,128)(2,1)}, bf16[4,128,128]{2,1,0:T(8,128)(2,1)S(1)}, u32[]{:S(2)}, u32[]{:S(2)}) collective-permute-start(bf16[4,128,128]{2,1,0:T(8,128)(2,1)} %get-tuple-element.81), channel_id=1, source_target_pairs={{0,96},{32,128},{64,160},{96,192},{128,224},{160,0},{192,32},{224,... | collective-permute-start | bytes 393224 | tf_op jit(solution)/shard_map/ppermute | solution.py:202
  91.2 2.3 %collective-permute-start.11 = (bf16[4,128,128]{2,1,0:T(8,128)(2,1)}, bf16[4,128,128]{2,1,0:T(8,128)(2,1)S(1)}, u32[]{:S(2)}, u32[]{:S(2)}) collective-permute-start(bf16[4,128,128]{2,1,0:T(8,128)(2,1)} %get-tuple-element.82), channel_id=1, source_target_pairs={{0,128},{32,160},{64,192},{96,224},{128,0},{160,32},{192,64},{224,... | collective-permute-start | bytes 393224 | tf_op jit(solution)/shard_map/ppermute | solution.py:202
  93.5 2.8 %collective-permute-start.12 = (bf16[4,128,128]{2,1,0:T(8,128)(2,1)}, bf16[4,128,128]{2,1,0:T(8,128)(2,1)S(1)}, u32[]{:S(2)}, u32[]{:S(2)}) collective-permute-start(bf16[4,128,128]{2,1,0:T(8,128)(2,1)} %get-tuple-element.83), channel_id=1, source_target_pairs={{0,160},{32,192},{64,224},{96,0},{128,32},{160,64},{192,96},{224,1... | collective-permute-start | bytes 393224 | tf_op jit(solution)/shard_map/ppermute | solution.py:202
  97.4 2.4 %collective-permute-start.13 = (bf16[4,128,128]{2,1,0:T(8,128)(2,1)}, bf16[4,128,128]{2,1,0:T(8,128)(2,1)S(1)}, u32[]{:S(2)}, u32[]{:S(2)}) collective-permute-start(bf16[4,128,128]{2,1,0:T(8,128)(2,1)} %get-tuple-element.84), channel_id=1, source_target_pairs={{0,192},{32,224},{64,0},{96,32},{128,64},{160,96},{192,128},{224,1... | collective-permute-start | bytes 393224 | tf_op jit(solution)/shard_map/ppermute | solution.py:202
  99.8 8.1 %collective-permute-start.14 = (bf16[4,128,128]{2,1,0:T(8,128)(2,1)}, bf16[4,128,128]{2,1,0:T(8,128)(2,1)S(1)}, u32[]{:S(2)}, u32[]{:S(2)}) collective-permute-start(bf16[4,128,128]{2,1,0:T(8,128)(2,1)} %get-tuple-element.85), channel_id=1, source_target_pairs={{0,224},{32,0},{64,32},{96,64},{128,96},{160,128},{192,160},{224,1... | collective-permute-start | bytes 393224 | tf_op jit(solution)/shard_map/ppermute | solution.py:202
  107.9 2.3 %shard_map.86 = bf16[32,6,32,128]{3,2,1,0:T(8,128)(2,1)} custom-call(s32[1]{0:T(128)} %bitcast.1.z_ref, s32[512]{0:T(512)S(1)} %reshape.33.ids_ref, bf16[32,272,128]{2,1,0:T(8,128)(2,1)S(1)} %all-to-all-done.table_ref), custom_call_target="tpu_custom_call" | custom-call | tf_op jit(solution)/shard_map/pallas_call | solution.py:39
  111.9 5.0 %collective-permute-done.13.refs_4_ = bf16[4,128,128]{2,1,0:T(8,128)(2,1)S(1)} collective-permute-done((bf16[4,128,128]{2,1,0:T(8,128)(2,1)}, bf16[4,128,128]{2,1,0:T(8,128)(2,1)S(1)}, u32[]{:S(2)}, u32[]{:S(2)}) %collective-permute-start.13) | collective-permute-done | bytes 131104 | tf_op jit(solution)/shard_map/ppermute | solution.py:202
  117.8 7.4 %all-to-all-start.2 = ((bf16[32,6,32,128]{3,2,1,0:T(8,128)(2,1)}), bf16[32,6,32,128]{3,2,1,0:T(8,128)(2,1)S(1)}, u32[]{:S(2)}, u32[]{:S(2)}) async-start(bf16[32,6,32,128]{3,2,1,0:T(8,128)(2,1)} %shard_map.86), calls=%async_computation.2 | async-start | bytes 3145728 | tf_op jit(solution)/shard_map/all_to_all | solution.py:250
  125.3 4.0 %shard_map.90 = (bf16[4,128,128]{2,1,0:T(8,128)(2,1)}, bf16[4,128,128]{2,1,0:T(8,128)(2,1)}, bf16[4,128,128]{2,1,0:T(8,128)(2,1)}, bf16[4,128,128]{2,1,0:T(8,128)(2,1)}, bf16[4,128,128]{2,1,0:T(8,128)(2,1)}) custom-call(bf16[4,128,128]{2,1,0:T(8,128)(2,1)} %copy-done.15, bf16[4,128,128]{2,1,0:T(8,128)(2,1)} %copy-done.14, bf16[4,128,128]{2,1,0:T(8,128)(2,1)} %copy-done.17, ...), custom_call_target="tpu_custom_call" | custom-call | tf_op jit(solution)/shard_map/pallas_call | solution.py:39
  129.3 2.7 %collective-permute-start.21 = (bf16[4,128,128]{2,1,0:T(8,128)(2,1)}, bf16[4,128,128]{2,1,0:T(8,128)(2,1)S(1)}, u32[]{:S(2)}, u32[]{:S(2)}) collective-permute-start(bf16[4,128,128]{2,1,0:T(8,128)(2,1)} %get-tuple-element.108), channel_id=1, source_target_pairs={{0,64},{32,96},{64,128},{96,160},{128,192},{160,224},{192,0},{224,... | collective-permute-start | bytes 393224 | tf_op jit(solution)/shard_map/ppermute | solution.py:202
  133.4 2.8 %collective-permute-start.18 = (bf16[4,128,128]{2,1,0:T(8,128)(2,1)}, bf16[4,128,128]{2,1,0:T(8,128)(2,1)S(1)}, u32[]{:S(2)}, u32[]{:S(2)}) collective-permute-start(bf16[4,128,128]{2,1,0:T(8,128)(2,1)} %get-tuple-element.105), channel_id=1, source_target_pairs={{0,160},{32,192},{64,224},{96,0},{128,32},{160,64},{192,96},{224,1... | collective-permute-start | bytes 393224 | tf_op jit(solution)/shard_map/ppermute | solution.py:202
  138.8 2.7 %collective-permute-start.24 = (bf16[2,4,144,128]{3,2,1,0:T(8,128)(2,1)}, bf16[2,4,144,128]{3,2,1,0:T(8,128)(2,1)S(1)}, u32[]{:S(2)}, u32[]{:S(2)}) collective-permute-start(bf16[2,4,144,128]{3,2,1,0:T(8,128)(2,1)} %get-tuple-element.117), channel_id=1, source_target_pairs={{0,4},{2,6},{4,0},{6,2},{1,5},{3,7},{5,1},{7,3},{8,12},{10,14},{12... | collective-permute-start | bytes 884744 | tf_op jit(solution)/shard_map/ppermute | solution.py:202
  144.1 2.4 %collective-permute-start.19 = (bf16[4,128,128]{2,1,0:T(8,128)(2,1)}, bf16[4,128,128]{2,1,0:T(8,128)(2,1)S(1)}, u32[]{:S(2)}, u32[]{:S(2)}) collective-permute-start(bf16[4,128,128]{2,1,0:T(8,128)(2,1)} %get-tuple-element.106), channel_id=1, source_target_pairs={{0,128},{32,160},{64,192},{96,224},{128,0},{160,32},{192,64},{224,... | collective-permute-start | bytes 393224 | tf_op jit(solution)/shard_map/ppermute | solution.py:202
  146.5 3.1 %collective-permute-done.18.refs_3_ = bf16[4,128,128]{2,1,0:T(8,128)(2,1)S(1)} collective-permute-done((bf16[4,128,128]{2,1,0:T(8,128)(2,1)}, bf16[4,128,128]{2,1,0:T(8,128)(2,1)S(1)}, u32[]{:S(2)}, u32[]{:S(2)}) %collective-permute-start.18) | collective-permute-done | bytes 131104 | tf_op jit(solution)/shard_map/ppermute | solution.py:202
  149.6 4.5 %collective-permute-start.20 = (bf16[4,128,128]{2,1,0:T(8,128)(2,1)}, bf16[4,128,128]{2,1,0:T(8,128)(2,1)S(1)}, u32[]{:S(2)}, u32[]{:S(2)}) collective-permute-start(bf16[4,128,128]{2,1,0:T(8,128)(2,1)} %get-tuple-element.107), channel_id=1, source_target_pairs={{0,96},{32,128},{64,160},{96,192},{128,224},{160,0},{192,32},{224,... | collective-permute-start | bytes 393224 | tf_op jit(solution)/shard_map/ppermute | solution.py:202
  154.1 2.7 %shard_map.89 = (bf16[4,128,128]{2,1,0:T(8,128)(2,1)}, bf16[4,128,128]{2,1,0:T(8,128)(2,1)}, bf16[4,128,128]{2,1,0:T(8,128)(2,1)}) custom-call(bf16[4,128,128]{2,1,0:T(8,128)(2,1)} %get-tuple-element.92.refs_0_, bf16[4,128,128]{2,1,0:T(8,128)(2,1)} %copy-done.22, bf16[4,128,128]{2,1,0:T(8,128)(2,1)} %copy-done.23, bf16[4,4,2,6,32,128]{5,4,3,2,1,0:T(8,128)(2,1)S(1)} %bitcast.9), custom_call_target="tpu_custom_call" | custom-call | tf_op jit(solution)/shard_map/pallas_call | solution.py:39
  156.7 4.3 %collective-permute-start.16 = (bf16[4,128,128]{2,1,0:T(8,128)(2,1)}, bf16[4,128,128]{2,1,0:T(8,128)(2,1)S(1)}, u32[]{:S(2)}, u32[]{:S(2)}) collective-permute-start(bf16[4,128,128]{2,1,0:T(8,128)(2,1)} %get-tuple-element.97), channel_id=1, source_target_pairs={{0,224},{32,0},{64,32},{96,64},{128,96},{160,128},{192,160},{224,1... | collective-permute-start | bytes 393224 | tf_op jit(solution)/shard_map/ppermute | solution.py:202
  161.0 3.8 %collective-permute-start.22 = (bf16[4,128,128]{2,1,0:T(8,128)(2,1)}, bf16[4,128,128]{2,1,0:T(8,128)(2,1)S(1)}, u32[]{:S(2)}, u32[]{:S(2)}) collective-permute-start(bf16[4,128,128]{2,1,0:T(8,128)(2,1)} %get-tuple-element.114), channel_id=1, source_target_pairs={{0,32},{32,64},{64,96},{96,128},{128,160},{160,192},{192,224},{224... | collective-permute-start | bytes 393224 | tf_op jit(solution)/shard_map/ppermute | solution.py:202
  164.9 3.1 %collective-permute-done.22.refs_7_ = bf16[4,128,128]{2,1,0:T(8,128)(2,1)S(1)} collective-permute-done((bf16[4,128,128]{2,1,0:T(8,128)(2,1)}, bf16[4,128,128]{2,1,0:T(8,128)(2,1)S(1)}, u32[]{:S(2)}, u32[]{:S(2)}) %collective-permute-start.22) | collective-permute-done | bytes 131104 | tf_op jit(solution)/shard_map/ppermute | solution.py:202
  168.7 3.2 %shard_map.91 = bf16[128,4096]{1,0:T(8,128)(2,1)} custom-call(s32[1]{0:T(128)} %bitcast.me_ref, s32[1]{0:T(128)} %bitcast.1.z_ref, bf16[4,128,128]{2,1,0:T(8,128)(2,1)} %get-tuple-element.96.refs_0_, bf16[4,128,128]{2,1,0:T(8,128)(2,1)} %copy-done.20, bf16[4,128,128]{2,1,0:T(8,128)(2,1)} %copy-done.11, bf16[4,128,128]{2,1,0:T(8,128)(2,1)} %copy-done.12, ...), custom_call_target="tpu_custom_call" | custom-call | tf_op jit(solution)/shard_map/pallas_call | solution.py:39
  (95 shorter events, 31.7 us)
Async XLA Ops:
  2.5 2.9 %collective-permute-start = (bf16[8,128,512]{2,1,0:T(8,128)(2,1)}, bf16[8,128,512]{2,1,0:T(8,128)(2,1)S(1)}, u32[]{:S(2)}, u32[]{:S(2)}) collective-permute-start(bf16[8,128,512]{2,1,0:T(8,128)(2,1)} %broadcast_select_fusion), channel_id=1, source_target_pairs={{0,1},{1,0},{2,3},{3,2},{4,5},{5,4},{6,7},{7,6},{8,9},{9,8},{10,11... | collective-permute-start | bytes 3145736 | tf_op jit(solution)/shard_map/ppermute | solution.py:202
  7.3 63.9 %all-to-all-start = ((bf16[32,272,128]{2,1,0:T(8,128)(2,1)}), bf16[32,272,128]{2,1,0:T(8,128)(2,1)S(1)}, u32[]{:S(2)}, u32[]{:S(2)}) async-start(bf16[32,272,128]{2,1,0:T(8,128)(2,1)} %shard_map.82), calls=%async_computation | async-start | bytes 4456448 | tf_op jit(solution)/shard_map/all_to_all | solution.py:222
  19.0 42.5 %copy-start.6 = (f32[4]{0:T(128)S(1)}, f32[4]{0:T(128)}, u32[]{:S(2)}) copy-start(f32[4]{0:T(128)} %gate_ref.1) | copy-start | bytes 52
  23.4 12.4 %collective-permute-start.1 = (bf16[3,128,512]{2,1,0:T(8,128)(2,1)}, bf16[3,128,512]{2,1,0:T(8,128)(2,1)}, u32[]{:S(2)}, u32[]{:S(2)}) collective-permute-start(bf16[3,128,512]{2,1,0:T(8,128)(2,1)} %get-tuple-element.63), channel_id=1, source_target_pairs={{0,1},{1,2},{2,3},{3,4},{4,5},{5,6},{6,7},{7,0},{8,9},{9,10},{10,1... | collective-permute-start | bytes 1179656 | tf_op jit(solution)/shard_map/ppermute | solution.py:202
  23.4 14.2 %collective-permute-start.2 = (bf16[3,128,512]{2,1,0:T(8,128)(2,1)}, bf16[3,128,512]{2,1,0:T(8,128)(2,1)}, u32[]{:S(2)}, u32[]{:S(2)}) collective-permute-start(bf16[3,128,512]{2,1,0:T(8,128)(2,1)} %get-tuple-element.64), channel_id=1, source_target_pairs={{0,2},{1,3},{2,4},{3,5},{4,6},{5,7},{6,0},{7,1},{8,10},{9,11},{10,... | collective-permute-start | bytes 1179656 | tf_op jit(solution)/shard_map/ppermute | solution.py:202
  25.0 28.9 %collective-permute-start.3 = (bf16[3,128,512]{2,1,0:T(8,128)(2,1)}, bf16[3,128,512]{2,1,0:T(8,128)(2,1)}, u32[]{:S(2)}, u32[]{:S(2)}) collective-permute-start(bf16[3,128,512]{2,1,0:T(8,128)(2,1)} %get-tuple-element.65), channel_id=1, source_target_pairs={{0,3},{1,4},{2,5},{3,6},{4,7},{5,0},{6,1},{7,2},{8,11},{9,12},{10,... | collective-permute-start | bytes 1179656 | tf_op jit(solution)/shard_map/ppermute | solution.py:202
  27.2 27.7 %collective-permute-start.4 = (bf16[3,128,512]{2,1,0:T(8,128)(2,1)}, bf16[3,128,512]{2,1,0:T(8,128)(2,1)}, u32[]{:S(2)}, u32[]{:S(2)}) collective-permute-start(bf16[3,128,512]{2,1,0:T(8,128)(2,1)} %get-tuple-element.66), channel_id=1, source_target_pairs={{0,4},{1,5},{2,6},{3,7},{4,0},{5,1},{6,2},{7,3},{8,12},{9,13},{10,... | collective-permute-start | bytes 1179656 | tf_op jit(solution)/shard_map/ppermute | solution.py:202
  29.1 30.4 %collective-permute-start.5 = (bf16[3,128,512]{2,1,0:T(8,128)(2,1)}, bf16[3,128,512]{2,1,0:T(8,128)(2,1)}, u32[]{:S(2)}, u32[]{:S(2)}) collective-permute-start(bf16[3,128,512]{2,1,0:T(8,128)(2,1)} %get-tuple-element.67), channel_id=1, source_target_pairs={{0,5},{1,6},{2,7},{3,0},{4,1},{5,2},{6,3},{7,4},{8,13},{9,14},{10,... | collective-permute-start | bytes 1179656 | tf_op jit(solution)/shard_map/ppermute | solution.py:202
  35.7 23.8 %collective-permute-start.6 = (bf16[3,128,512]{2,1,0:T(8,128)(2,1)}, bf16[3,128,512]{2,1,0:T(8,128)(2,1)}, u32[]{:S(2)}, u32[]{:S(2)}) collective-permute-start(bf16[3,128,512]{2,1,0:T(8,128)(2,1)} %get-tuple-element.68), channel_id=1, source_target_pairs={{0,6},{1,7},{2,0},{3,1},{4,2},{5,3},{6,4},{7,5},{8,14},{9,15},{10,... | collective-permute-start | bytes 1179656 | tf_op jit(solution)/shard_map/ppermute | solution.py:202
  37.6 23.9 %collective-permute-start.7 = (bf16[3,128,512]{2,1,0:T(8,128)(2,1)}, bf16[3,128,512]{2,1,0:T(8,128)(2,1)}, u32[]{:S(2)}, u32[]{:S(2)}) collective-permute-start(bf16[3,128,512]{2,1,0:T(8,128)(2,1)} %get-tuple-element.69), channel_id=1, source_target_pairs={{0,7},{1,0},{2,1},{3,2},{4,3},{5,4},{6,5},{7,6},{8,15},{9,8},{10,9... | collective-permute-start | bytes 1179656 | tf_op jit(solution)/shard_map/ppermute | solution.py:202
  75.0 42.8 %all-to-all-start.1 = ((bf16[32,10,32,128]{3,2,1,0:T(8,128)(2,1)}), bf16[32,10,32,128]{3,2,1,0:T(8,128)(2,1)}, u32[]{:S(2)}, u32[]{:S(2)}) async-start(bf16[32,10,32,128]{3,2,1,0:T(8,128)(2,1)} %shard_map.85), calls=%async_computation.1 | async-start | bytes 5242880 | tf_op jit(solution)/shard_map/all_to_all | solution.py:250
  83.1 27.2 %copy-start.5 = (bf16[4,4,144,128]{3,2,1,0:T(8,128)(2,1)S(1)}, bf16[4,4,144,128]{3,2,1,0:T(8,128)(2,1)}, u32[]{:S(2)}) copy-start(bf16[4,4,144,128]{3,2,1,0:T(8,128)(2,1)} %get-tuple-element.86.own_ref) | copy-start | bytes 1769476
  83.1 16.7 %collective-permute-start.15 = (bf16[4,4,144,128]{3,2,1,0:T(8,128)(2,1)}, bf16[4,4,144,128]{3,2,1,0:T(8,128)(2,1)S(1)}, u32[]{:S(2)}, u32[]{:S(2)}) collective-permute-start(bf16[4,4,144,128]{3,2,1,0:T(8,128)(2,1)} %get-tuple-element.87), channel_id=1, source_target_pairs={{0,1},{1,0},{2,3},{3,2},{4,5},{5,4},{6,7},{7,6},{8,9},{9,8},{10,11... | collective-permute-start | bytes 1769480 | tf_op jit(solution)/shard_map/ppermute | solution.py:202
  84.6 8.9 %collective-permute-start.8 = (bf16[4,128,128]{2,1,0:T(8,128)(2,1)}, bf16[4,128,128]{2,1,0:T(8,128)(2,1)S(1)}, u32[]{:S(2)}, u32[]{:S(2)}) collective-permute-start(bf16[4,128,128]{2,1,0:T(8,128)(2,1)} %get-tuple-element.79), channel_id=1, source_target_pairs={{0,32},{32,64},{64,96},{96,128},{128,160},{160,192},{192,224},{224... | collective-permute-start | bytes 393224 | tf_op jit(solution)/shard_map/ppermute | solution.py:202
  86.3 11.1 %collective-permute-start.9 = (bf16[4,128,128]{2,1,0:T(8,128)(2,1)}, bf16[4,128,128]{2,1,0:T(8,128)(2,1)S(1)}, u32[]{:S(2)}, u32[]{:S(2)}) collective-permute-start(bf16[4,128,128]{2,1,0:T(8,128)(2,1)} %get-tuple-element.80), channel_id=1, source_target_pairs={{0,64},{32,96},{64,128},{96,160},{128,192},{160,224},{192,0},{224,... | collective-permute-start | bytes 393224 | tf_op jit(solution)/shard_map/ppermute | solution.py:202
  88.5 22.9 %collective-permute-start.10 = (bf16[4,128,128]{2,1,0:T(8,128)(2,1)}, bf16[4,128,128]{2,1,0:T(8,128)(2,1)S(1)}, u32[]{:S(2)}, u32[]{:S(2)}) collective-permute-start(bf16[4,128,128]{2,1,0:T(8,128)(2,1)} %get-tuple-element.81), channel_id=1, source_target_pairs={{0,96},{32,128},{64,160},{96,192},{128,224},{160,0},{192,32},{224,... | collective-permute-start | bytes 393224 | tf_op jit(solution)/shard_map/ppermute | solution.py:202
  91.2 20.2 %collective-permute-start.11 = (bf16[4,128,128]{2,1,0:T(8,128)(2,1)}, bf16[4,128,128]{2,1,0:T(8,128)(2,1)S(1)}, u32[]{:S(2)}, u32[]{:S(2)}) collective-permute-start(bf16[4,128,128]{2,1,0:T(8,128)(2,1)} %get-tuple-element.82), channel_id=1, source_target_pairs={{0,128},{32,160},{64,192},{96,224},{128,0},{160,32},{192,64},{224,... | collective-permute-start | bytes 393224 | tf_op jit(solution)/shard_map/ppermute | solution.py:202
  93.5 18.4 %collective-permute-start.12 = (bf16[4,128,128]{2,1,0:T(8,128)(2,1)}, bf16[4,128,128]{2,1,0:T(8,128)(2,1)S(1)}, u32[]{:S(2)}, u32[]{:S(2)}) collective-permute-start(bf16[4,128,128]{2,1,0:T(8,128)(2,1)} %get-tuple-element.83), channel_id=1, source_target_pairs={{0,160},{32,192},{64,224},{96,0},{128,32},{160,64},{192,96},{224,1... | collective-permute-start | bytes 393224 | tf_op jit(solution)/shard_map/ppermute | solution.py:202
  97.4 19.5 %collective-permute-start.13 = (bf16[4,128,128]{2,1,0:T(8,128)(2,1)}, bf16[4,128,128]{2,1,0:T(8,128)(2,1)S(1)}, u32[]{:S(2)}, u32[]{:S(2)}) collective-permute-start(bf16[4,128,128]{2,1,0:T(8,128)(2,1)} %get-tuple-element.84), channel_id=1, source_target_pairs={{0,192},{32,224},{64,0},{96,32},{128,64},{160,96},{192,128},{224,1... | collective-permute-start | bytes 393224 | tf_op jit(solution)/shard_map/ppermute | solution.py:202
  99.8 18.0 %collective-permute-start.14 = (bf16[4,128,128]{2,1,0:T(8,128)(2,1)}, bf16[4,128,128]{2,1,0:T(8,128)(2,1)S(1)}, u32[]{:S(2)}, u32[]{:S(2)}) collective-permute-start(bf16[4,128,128]{2,1,0:T(8,128)(2,1)} %get-tuple-element.85), channel_id=1, source_target_pairs={{0,224},{32,0},{64,32},{96,64},{128,96},{160,128},{192,160},{224,1... | collective-permute-start | bytes 393224 | tf_op jit(solution)/shard_map/ppermute | solution.py:202
  117.8 36.2 %all-to-all-start.2 = ((bf16[32,6,32,128]{3,2,1,0:T(8,128)(2,1)}), bf16[32,6,32,128]{3,2,1,0:T(8,128)(2,1)S(1)}, u32[]{:S(2)}, u32[]{:S(2)}) async-start(bf16[32,6,32,128]{3,2,1,0:T(8,128)(2,1)} %shard_map.86), calls=%async_computation.2 | async-start | bytes 3145728 | tf_op jit(solution)/shard_map/all_to_all | solution.py:250
  129.3 8.0 %collective-permute-start.21 = (bf16[4,128,128]{2,1,0:T(8,128)(2,1)}, bf16[4,128,128]{2,1,0:T(8,128)(2,1)S(1)}, u32[]{:S(2)}, u32[]{:S(2)}) collective-permute-start(bf16[4,128,128]{2,1,0:T(8,128)(2,1)} %get-tuple-element.108), channel_id=1, source_target_pairs={{0,64},{32,96},{64,128},{96,160},{128,192},{160,224},{192,0},{224,... | collective-permute-start | bytes 393224 | tf_op jit(solution)/shard_map/ppermute | solution.py:202
  131.9 12.1 %collective-permute-start.17 = (bf16[4,128,128]{2,1,0:T(8,128)(2,1)}, bf16[4,128,128]{2,1,0:T(8,128)(2,1)S(1)}, u32[]{:S(2)}, u32[]{:S(2)}) collective-permute-start(bf16[4,128,128]{2,1,0:T(8,128)(2,1)} %get-tuple-element.104), channel_id=1, source_target_pairs={{0,192},{32,224},{64,0},{96,32},{128,64},{160,96},{192,128},{224,1... | collective-permute-start | bytes 393224 | tf_op jit(solution)/shard_map/ppermute | solution.py:202
  133.4 16.2 %collective-permute-start.18 = (bf16[4,128,128]{2,1,0:T(8,128)(2,1)}, bf16[4,128,128]{2,1,0:T(8,128)(2,1)S(1)}, u32[]{:S(2)}, u32[]{:S(2)}) collective-permute-start(bf16[4,128,128]{2,1,0:T(8,128)(2,1)} %get-tuple-element.105), channel_id=1, source_target_pairs={{0,160},{32,192},{64,224},{96,0},{128,32},{160,64},{192,96},{224,1... | collective-permute-start | bytes 393224 | tf_op jit(solution)/shard_map/ppermute | solution.py:202
  137.3 30.8 %copy-start.10 = (bf16[4,128,128]{2,1,0:T(8,128)(2,1)}, bf16[4,128,128]{2,1,0:T(8,128)(2,1)S(1)}, u32[]{:S(2)}) copy-start(bf16[4,128,128]{2,1,0:T(8,128)(2,1)S(1)} %collective-permute-done.21.refs_6_) | copy-start | bytes 393220
  137.3 27.6 %collective-permute-start.23 = (bf16[2,4,144,128]{3,2,1,0:T(8,128)(2,1)}, bf16[2,4,144,128]{3,2,1,0:T(8,128)(2,1)S(1)}, u32[]{:S(2)}, u32[]{:S(2)}) collective-permute-start(bf16[2,4,144,128]{3,2,1,0:T(8,128)(2,1)} %get-tuple-element.116), channel_id=1, source_target_pairs={{0,2},{2,4},{4,6},{6,0},{1,3},{3,5},{5,7},{7,1},{8,10},{10,12},{12... | collective-permute-start | bytes 884744 | tf_op jit(solution)/shard_map/ppermute | solution.py:202
  138.8 26.1 %collective-permute-start.24 = (bf16[2,4,144,128]{3,2,1,0:T(8,128)(2,1)}, bf16[2,4,144,128]{3,2,1,0:T(8,128)(2,1)S(1)}, u32[]{:S(2)}, u32[]{:S(2)}) collective-permute-start(bf16[2,4,144,128]{3,2,1,0:T(8,128)(2,1)} %get-tuple-element.117), channel_id=1, source_target_pairs={{0,4},{2,6},{4,0},{6,2},{1,5},{3,7},{5,1},{7,3},{8,12},{10,14},{12... | collective-permute-start | bytes 884744 | tf_op jit(solution)/shard_map/ppermute | solution.py:202
  141.5 23.4 %collective-permute-start.25 = (bf16[2,4,144,128]{3,2,1,0:T(8,128)(2,1)}, bf16[2,4,144,128]{3,2,1,0:T(8,128)(2,1)S(1)}, u32[]{:S(2)}, u32[]{:S(2)}) collective-permute-start(bf16[2,4,144,128]{3,2,1,0:T(8,128)(2,1)} %get-tuple-element.118), channel_id=1, source_target_pairs={{0,6},{2,0},{4,2},{6,4},{1,7},{3,1},{5,3},{7,5},{8,14},{10,8},{12,... | collective-permute-start | bytes 884744 | tf_op jit(solution)/shard_map/ppermute | solution.py:202
  144.1 12.7 %collective-permute-start.19 = (bf16[4,128,128]{2,1,0:T(8,128)(2,1)}, bf16[4,128,128]{2,1,0:T(8,128)(2,1)S(1)}, u32[]{:S(2)}, u32[]{:S(2)}) collective-permute-start(bf16[4,128,128]{2,1,0:T(8,128)(2,1)} %get-tuple-element.106), channel_id=1, source_target_pairs={{0,128},{32,160},{64,192},{96,224},{128,0},{160,32},{192,64},{224,... | collective-permute-start | bytes 393224 | tf_op jit(solution)/shard_map/ppermute | solution.py:202
  149.6 11.4 %collective-permute-start.20 = (bf16[4,128,128]{2,1,0:T(8,128)(2,1)}, bf16[4,128,128]{2,1,0:T(8,128)(2,1)S(1)}, u32[]{:S(2)}, u32[]{:S(2)}) collective-permute-start(bf16[4,128,128]{2,1,0:T(8,128)(2,1)} %get-tuple-element.107), channel_id=1, source_target_pairs={{0,96},{32,128},{64,160},{96,192},{128,224},{160,0},{192,32},{224,... | collective-permute-start | bytes 393224 | tf_op jit(solution)/shard_map/ppermute | solution.py:202
  156.7 8.2 %collective-permute-start.16 = (bf16[4,128,128]{2,1,0:T(8,128)(2,1)}, bf16[4,128,128]{2,1,0:T(8,128)(2,1)S(1)}, u32[]{:S(2)}, u32[]{:S(2)}) collective-permute-start(bf16[4,128,128]{2,1,0:T(8,128)(2,1)} %get-tuple-element.97), channel_id=1, source_target_pairs={{0,224},{32,0},{64,32},{96,64},{128,96},{160,128},{192,160},{224,1... | collective-permute-start | bytes 393224 | tf_op jit(solution)/shard_map/ppermute | solution.py:202
  161.0 7.0 %collective-permute-start.22 = (bf16[4,128,128]{2,1,0:T(8,128)(2,1)}, bf16[4,128,128]{2,1,0:T(8,128)(2,1)S(1)}, u32[]{:S(2)}, u32[]{:S(2)}) collective-permute-start(bf16[4,128,128]{2,1,0:T(8,128)(2,1)} %get-tuple-element.114), channel_id=1, source_target_pairs={{0,32},{32,64},{64,96},{96,128},{128,160},{160,192},{192,224},{224... | collective-permute-start | bytes 393224 | tf_op jit(solution)/shard_map/ppermute | solution.py:202
  (23 other events, 196.7 us)

commit v3 on v2

--- a/solution.py
+++ b/solution.py
@@ -57,14 +57,13 @@
     return lax.dot_general(a, b, (((1,), (1,)), ((), ())), preferred_element_type=jnp.float32)
 
 
-def spread_kernel(core_ref, keys_ref, values_ref, swapped_ref, ids_ref, out_ref):
+def spread_kernel(core_ref, keys_ref, swapped_ref, ids_ref, out_ref):
     core = core_ref[0]
-    for j in range(HEADS_DEV):
-        for x in range(BLK // ROWS):
-            rows, cols = pl.ds(x * ROWS, ROWS), pl.ds(j * DH, DH)
-            kept = jnp.where(core == 0, keys_ref[:, rows, cols], values_ref[:, rows, cols])
-            for source, piece in ((core, kept), (1 - core, swapped_ref[:, rows, cols])):
+    for source, ref in ((core, keys_ref), (1 - core, swapped_ref)):
+        for j in range(HEADS_DEV):
+            for x in range(BLK // ROWS):
                 dest = (source * HEADS_DEV + j) * (BLK // ROWS) + x
+                piece = ref[:, pl.ds(x * ROWS, ROWS), pl.ds(j * DH, DH)]
                 out_ref[dest, pl.ds(0, SLOTS * ROWS), :] = piece.reshape(SLOTS * ROWS, DH)
     for dest in range(MEM_DEVS):
         out_ref[dest, pl.ds(SLOTS * ROWS, TAIL), :] = ids_ref[...]
@@ -92,12 +91,13 @@
             out_refs[shift][y] = q_ref[:, cols]
 
 
-def attend_kernel(count, *refs):
+def attend_kernel(count, z_ref, *refs):
+    core = z_ref[0] // HEADS_DEV
     queries, fetched_ref, outs = refs[:count], refs[count], refs[count + 1 :]
     for i in range(count):
         for y in range(HEADS_DEV):
-            keys = fetched_ref[:, y, 0, pl.ds(2 * i, 2)].reshape(2 * BLK, DH)
-            values = fetched_ref[:, y, 1, pl.ds(2 * i, 2)].reshape(2 * BLK, DH)
+            keys = fetched_ref[:, y, core, pl.ds(2 * i, 2)].reshape(2 * BLK, DH)
+            values = fetched_ref[:, y, 1 - core, pl.ds(2 * i, 2)].reshape(2 * BLK, DH)
             scores = dot_nt(queries[i][y], keys)
             top = jnp.max(scores, axis=1, keepdims=True)
             weights = jnp.exp2((scores - top) * EXP_SCALE)
@@ -210,14 +210,14 @@
     me = lax.axis_index(("y", "c")).astype(jnp.int32).reshape(1)
     query = query_rows[0]
 
-    swapped = shifted(jnp.where(core == 0, memory_values, memory_keys), "c", CORES, 1)
+    swapped = shifted(memory_values, "c", CORES, 1)
     ids = (owner_list * SLOTS + slot_list).reshape(TAIL, 1)
     ids = jnp.broadcast_to(ids.astype(jnp.bfloat16), (TAIL, DH))
     (spread,) = call(
         spread_kernel,
         [(MEM_DEVS, SLOTS * ROWS + TAIL, DH)],
         [core.astype(jnp.int32).reshape(1)],
-        [memory_keys, memory_values, swapped, ids],
+        [memory_keys, swapped, ids],
     )
     table = lax.all_to_all(spread, ("z", "x"), split_axis=0, concat_axis=0, tiled=True)
 
@@ -234,7 +234,8 @@
         24,
         range(HEAD_DEVS),
     )
-    table, local = lax.optimization_barrier((table, local))
+    asked = call(query_kernel, [(HEADS_DEV, BLK, DH)] * PLANES, [z], [query])
+    table, local, asked = lax.optimization_barrier((table, local, asked))
 
     all_ids = table[:, SLOTS * ROWS :, 0].astype(jnp.int32).reshape(MEM_DEVS * TAIL)
 
@@ -256,22 +257,22 @@
         return call(
             functools.partial(attend_kernel, len(shifts)),
             [(HEADS_DEV, BLK, DH)] * len(shifts),
-            [],
+            [z],
             [asked[s] for s in shifts] + [fetched],
             hbm=range(len(shifts)),
         )
 
-    far, table, query, local = lax.optimization_barrier((gathered(FAR, table), table, query, local))
+    far, table, asked, local = lax.optimization_barrier((gathered(FAR, table), table, asked, local))
     far = fetch(far)
     near = gathered(NEAR, table)
     local = [local[0], shifted(local[1], "c", CORES, 1)]
     local = call(merge_kernel, [(CORES, HEADS_DEV, BLK + TAIL, DH)] * CHIPS, [me], local)
-    asked = call(query_kernel, [(HEADS_DEV, BLK, DH)] * PLANES, [z], [query])
-    asked = [shifted(asked[s], "z", PLANES, s) for s in range(PLANES)]
+    asked = {s: shifted(asked[s], "z", PLANES, s) for s in FAR + NEAR}
     far, near, asked, local = lax.optimization_barrier((far, near, asked, local))
 
+    parts, near = lax.optimization_barrier((attend(FAR, far), near))
     near = fetch(near)
-    memory = {s: shifted(part, "z", PLANES, -s) for s, part in zip(FAR, attend(FAR, far))}
+    memory = {s: shifted(part, "z", PLANES, -s) for s, part in zip(FAR, parts)}
     memory[6], local = lax.optimization_barrier((memory[6], local))
     local = [shifted(local[s], "y", CHIPS, s) for s in range(CHIPS)]
     memory.update({s: shifted(part, "z", PLANES, -s) for s, part in zip(NEAR, attend(NEAR, near))})

time: 174 us -> 170 us (0.977); the launches traced: 172 us -> 170 us
  starting transfers between devices: 94.5 us -> 91.7 us
  other arithmetic: 3.08 us -> 1.32 us
    ppermute x26, starting transfers between devices: 67.4 us -> 64.3 us  [shifted(): lax.ppermute(array, axis, [(i, (i + shift) % size) for i in range(size)])]
    select_n x1 -> x0, other arithmetic: 2.46 us -> none  [on_device(): jnp.where(core == 0, memory_values, memory_keys)]
    unnamed x52 -> x64, local copies, waits for them, and re-layouts: 3.11 us -> 4.39 us
  transfers between devices with their start and end apart: 29 -> 29, of which waited for: 15 -> 17; matrix products, arithmetic and copies ran while one was open for 0% -> 1% of each run, Pallas kernels for 13% -> 11%
where the time goes in v3:
time: 170 us
  starting transfers between devices  91.7 us (54%)
  waiting for transfers between devices  41.1 us (24%)
  Pallas kernels  30.8 us (18%)
  local copies, waits for them, and re-layouts  4.72 us (3%)
    ppermute x26, starting transfers between devices, shifted(): lax.ppermute(array, axis, [(i, (i + shift) % size) for i in range(size)])  64.3 us
    ppermute x26, waiting for transfers between devices, shifted(): lax.ppermute(array, axis, [(i, (i + shift) % size) for i in range(size)])  40.1 us
    pallas_call x10, Pallas kernels, call(): pl.pallas_call(kernel, out_shape=outs, grid=(1,), in_specs=[pl.BlockSpec(...  30.8 us
    all_to_all x2, starting transfers between devices, fetch(): lax.all_to_all(requested, ('x', 'y', 'c'), split_axis=0, concat_axis=0, t...  15.7 us
    all_to_all x1, starting transfers between devices, on_device(): lax.all_to_all(spread, ('z', 'x'), split_axis=0, concat_axis=0, tiled=True)  11.7 us
    unnamed x64, local copies, waits for them, and re-layouts  4.39 us
  transfers between devices with their start and end apart: 29, of which 17 were waited for; matrix products, arithmetic and copies ran while one was open for 1% of the time, Pallas kernels for 11%

profile of v3, /device:TPU:6, one launch (start us, length us, event | category | flops | bytes accessed | tf_op | source)
XLA Modules:
  0.0 169.8 jit_solution(6633119282238726986)
XLA Ops:
  0.9 2.0 %collective-permute-done.swapped_ref = bf16[8,128,512]{2,1,0:T(8,128)(2,1)S(1)} collective-permute-done((bf16[8,128,512]{2,1,0:T(8,128)(2,1)}, bf16[8,128,512]{2,1,0:T(8,128)(2,1)S(1)}, u32[]{:S(2)}, u32[]{:S(2)}) %collective-permute-start) | collective-permute-done | bytes 1048608 | tf_op jit(solution)/shard_map/ppermute | solution.py:202
  5.9 11.7 %all-to-all-start = ((bf16[32,272,128]{2,1,0:T(8,128)(2,1)}), bf16[32,272,128]{2,1,0:T(8,128)(2,1)S(1)}, u32[]{:S(2)}, u32[]{:S(2)}) async-start(bf16[32,272,128]{2,1,0:T(8,128)(2,1)} %shard_map.82), calls=%async_computation | async-start | bytes 4456448 | tf_op jit(solution)/shard_map/all_to_all | solution.py:222
  23.6 2.3 %collective-permute-start.3 = (bf16[3,128,512]{2,1,0:T(8,128)(2,1)}, bf16[3,128,512]{2,1,0:T(8,128)(2,1)}, u32[]{:S(2)}, u32[]{:S(2)}) collective-permute-start(bf16[3,128,512]{2,1,0:T(8,128)(2,1)} %get-tuple-element.86), channel_id=1, source_target_pairs={{0,3},{1,4},{2,5},{3,6},{4,7},{5,0},{6,1},{7,2},{8,11},{9,12},{10,... | collective-permute-start | bytes 1179656 | tf_op jit(solution)/shard_map/ppermute | solution.py:202
  29.5 4.9 %collective-permute-done.1.refs_1_ = bf16[3,128,512]{2,1,0:T(8,128)(2,1)} collective-permute-done((bf16[3,128,512]{2,1,0:T(8,128)(2,1)}, bf16[3,128,512]{2,1,0:T(8,128)(2,1)}, u32[]{:S(2)}, u32[]{:S(2)}) %collective-permute-start.1) | collective-permute-done | bytes 393248 | tf_op jit(solution)/shard_map/ppermute | solution.py:202
  36.2 8.1 %collective-permute-start.7 = (bf16[3,128,512]{2,1,0:T(8,128)(2,1)}, bf16[3,128,512]{2,1,0:T(8,128)(2,1)}, u32[]{:S(2)}, u32[]{:S(2)}) collective-permute-start(bf16[3,128,512]{2,1,0:T(8,128)(2,1)} %get-tuple-element.90), channel_id=1, source_target_pairs={{0,7},{1,0},{2,1},{3,2},{4,3},{5,4},{6,5},{7,6},{8,15},{9,8},{10,9... | collective-permute-start | bytes 1179656 | tf_op jit(solution)/shard_map/ppermute | solution.py:202
  45.7 6.8 %collective-permute-done.3.refs_3_ = bf16[3,128,512]{2,1,0:T(8,128)(2,1)} collective-permute-done((bf16[3,128,512]{2,1,0:T(8,128)(2,1)}, bf16[3,128,512]{2,1,0:T(8,128)(2,1)}, u32[]{:S(2)}, u32[]{:S(2)}) %collective-permute-start.3) | collective-permute-done | bytes 393248 | tf_op jit(solution)/shard_map/ppermute | solution.py:202
  53.6 4.6 %collective-permute-done.5.refs_5_ = bf16[3,128,512]{2,1,0:T(8,128)(2,1)} collective-permute-done((bf16[3,128,512]{2,1,0:T(8,128)(2,1)}, bf16[3,128,512]{2,1,0:T(8,128)(2,1)}, u32[]{:S(2)}, u32[]{:S(2)}) %collective-permute-start.5) | collective-permute-done | bytes 393248 | tf_op jit(solution)/shard_map/ppermute | solution.py:202
  60.1 9.5 %shard_map.84 = (bf16[4,4,144,128]{3,2,1,0:T(8,128)(2,1)}, bf16[4,4,144,128]{3,2,1,0:T(8,128)(2,1)}) custom-call(s32[1]{0:T(128)} %bitcast.me_ref, f32[4]{0:T(128)S(1)} %copy-done.5, bf16[3,128,512]{2,1,0:T(8,128)(2,1)} %get-tuple-element.83.refs_0_, bf16[3,128,512]{2,1,0:T(8,128)(2,1)} %collective-permute-done.1.refs_1_, ...), custom_call_target="tpu_custom_call" | custom-call | tf_op jit(solution)/shard_map/pallas_call | solution.py:39
  70.5 3.1 %shard_map.86 = bf16[32,10,32,128]{3,2,1,0:T(8,128)(2,1)} custom-call(s32[1]{0:T(128)} %bitcast.1.z_ref, s32[512]{0:T(512)S(1)} %reshape.33.ids_ref, bf16[32,272,128]{2,1,0:T(8,128)(2,1)S(1)} %all-to-all-done.table_ref), custom_call_target="tpu_custom_call" | custom-call | tf_op jit(solution)/shard_map/pallas_call | solution.py:39
  73.6 8.2 %all-to-all-start.1 = ((bf16[32,10,32,128]{3,2,1,0:T(8,128)(2,1)}), bf16[32,10,32,128]{3,2,1,0:T(8,128)(2,1)}, u32[]{:S(2)}, u32[]{:S(2)}) async-start(bf16[32,10,32,128]{3,2,1,0:T(8,128)(2,1)} %shard_map.86), calls=%async_computation.1 | async-start | bytes 5242880 | tf_op jit(solution)/shard_map/all_to_all | solution.py:251
  82.1 3.3 %collective-permute-start.10 = (bf16[4,128,128]{2,1,0:T(8,128)(2,1)S(1)}, bf16[4,128,128]{2,1,0:T(8,128)(2,1)S(1)}, u32[]{:S(2)}, u32[]{:S(2)}) collective-permute-start(bf16[4,128,128]{2,1,0:T(8,128)(2,1)S(1)} %copy-done.28), channel_id=1, source_target_pairs={{0,96},{32,128},{64,160},{96,192},{128,224},{160,0},{192,32},{224,... | collective-permute-start | bytes 393224 | tf_op jit(solution)/shard_map/ppermute | solution.py:202
  85.4 2.7 %collective-permute-start.11 = (bf16[4,128,128]{2,1,0:T(8,128)(2,1)S(1)}, bf16[4,128,128]{2,1,0:T(8,128)(2,1)S(1)}, u32[]{:S(2)}, u32[]{:S(2)}) collective-permute-start(bf16[4,128,128]{2,1,0:T(8,128)(2,1)S(1)} %copy-done.26), channel_id=1, source_target_pairs={{0,128},{32,160},{64,192},{96,224},{128,0},{160,32},{192,64},{224,... | collective-permute-start | bytes 393224 | tf_op jit(solution)/shard_map/ppermute | solution.py:202
  88.1 4.4 %collective-permute-start.12 = (bf16[4,128,128]{2,1,0:T(8,128)(2,1)}, bf16[4,128,128]{2,1,0:T(8,128)(2,1)S(1)}, u32[]{:S(2)}, u32[]{:S(2)}) collective-permute-start(bf16[4,128,128]{2,1,0:T(8,128)(2,1)} %get-tuple-element.119), channel_id=1, source_target_pairs={{0,160},{32,192},{64,224},{96,0},{128,32},{160,64},{192,96},{224,1... | collective-permute-start | bytes 393224 | tf_op jit(solution)/shard_map/ppermute | solution.py:202
  93.1 2.9 %collective-permute-done.10.refs_1_ = bf16[4,128,128]{2,1,0:T(8,128)(2,1)S(1)} collective-permute-done((bf16[4,128,128]{2,1,0:T(8,128)(2,1)S(1)}, bf16[4,128,128]{2,1,0:T(8,128)(2,1)S(1)}, u32[]{:S(2)}, u32[]{:S(2)}) %collective-permute-start.10) | collective-permute-done | bytes 131104 | tf_op jit(solution)/shard_map/ppermute | solution.py:202
  96.0 2.2 %collective-permute-start.14 = (bf16[4,128,128]{2,1,0:T(8,128)(2,1)}, bf16[4,128,128]{2,1,0:T(8,128)(2,1)S(1)}, u32[]{:S(2)}, u32[]{:S(2)}) collective-permute-start(bf16[4,128,128]{2,1,0:T(8,128)(2,1)} %get-tuple-element.121), channel_id=1, source_target_pairs={{0,224},{32,0},{64,32},{96,64},{128,96},{160,128},{192,160},{224,1... | collective-permute-start | bytes 393224 | tf_op jit(solution)/shard_map/ppermute | solution.py:202
  99.9 3.1 %collective-permute-start.8 = (bf16[4,128,128]{2,1,0:T(8,128)(2,1)S(1)}, bf16[4,128,128]{2,1,0:T(8,128)(2,1)S(1)}, u32[]{:S(2)}, u32[]{:S(2)}) collective-permute-start(bf16[4,128,128]{2,1,0:T(8,128)(2,1)S(1)} %copy-done.25), channel_id=1, source_target_pairs={{0,32},{32,64},{64,96},{96,128},{128,160},{160,192},{192,224},{224... | collective-permute-start | bytes 393224 | tf_op jit(solution)/shard_map/ppermute | solution.py:202
  104.8 2.3 %shard_map.87 = bf16[32,6,32,128]{3,2,1,0:T(8,128)(2,1)} custom-call(s32[1]{0:T(128)} %bitcast.1.z_ref, s32[512]{0:T(512)S(1)} %reshape.33.ids_ref, bf16[32,272,128]{2,1,0:T(8,128)(2,1)S(1)} %all-to-all-done.table_ref), custom_call_target="tpu_custom_call" | custom-call | tf_op jit(solution)/shard_map/pallas_call | solution.py:39
  108.2 2.6 %collective-permute-done.13.refs_4_ = bf16[4,128,128]{2,1,0:T(8,128)(2,1)S(1)} collective-permute-done((bf16[4,128,128]{2,1,0:T(8,128)(2,1)}, bf16[4,128,128]{2,1,0:T(8,128)(2,1)S(1)}, u32[]{:S(2)}, u32[]{:S(2)}) %collective-permute-start.13) | collective-permute-done | bytes 131104 | tf_op jit(solution)/shard_map/ppermute | solution.py:202
  113.7 4.0 %shard_map.89 = (bf16[4,128,128]{2,1,0:T(8,128)(2,1)}, bf16[4,128,128]{2,1,0:T(8,128)(2,1)}, bf16[4,128,128]{2,1,0:T(8,128)(2,1)}, bf16[4,128,128]{2,1,0:T(8,128)(2,1)}, bf16[4,128,128]{2,1,0:T(8,128)(2,1)}) custom-call(s32[1]{0:T(128)} %bitcast.1.z_ref, bf16[4,128,128]{2,1,0:T(8,128)(2,1)} %copy-done.15, bf16[4,128,128]{2,1,0:T(8,128)(2,1)} %copy-done.14, ...), custom_call_target="tpu_custom_call" | custom-call | tf_op jit(solution)/shard_map/pallas_call | solution.py:39
  117.7 7.4 %all-to-all-start.2 = ((bf16[32,6,32,128]{3,2,1,0:T(8,128)(2,1)}), bf16[32,6,32,128]{3,2,1,0:T(8,128)(2,1)S(1)}, u32[]{:S(2)}, u32[]{:S(2)}) async-start(bf16[32,6,32,128]{3,2,1,0:T(8,128)(2,1)} %shard_map.87), calls=%async_computation.2 | async-start | bytes 3145728 | tf_op jit(solution)/shard_map/all_to_all | solution.py:251
  125.2 2.0 %collective-permute-start.21 = (bf16[4,128,128]{2,1,0:T(8,128)(2,1)S(1)}, bf16[4,128,128]{2,1,0:T(8,128)(2,1)S(1)}, u32[]{:S(2)}, u32[]{:S(2)}) collective-permute-start(bf16[4,128,128]{2,1,0:T(8,128)(2,1)S(1)} %copy-done.31), channel_id=1, source_target_pairs={{0,64},{32,96},{64,128},{96,160},{128,192},{160,224},{192,0},{224,... | collective-permute-start | bytes 393224 | tf_op jit(solution)/shard_map/ppermute | solution.py:202
  127.2 2.2 %collective-permute-start.17 = (bf16[4,128,128]{2,1,0:T(8,128)(2,1)S(1)}, bf16[4,128,128]{2,1,0:T(8,128)(2,1)S(1)}, u32[]{:S(2)}, u32[]{:S(2)}) collective-permute-start(bf16[4,128,128]{2,1,0:T(8,128)(2,1)S(1)} %copy-done.30), channel_id=1, source_target_pairs={{0,192},{32,224},{64,0},{96,32},{128,64},{160,96},{192,128},{224,1... | collective-permute-start | bytes 393224 | tf_op jit(solution)/shard_map/ppermute | solution.py:202
  129.4 4.4 %collective-permute-start.18 = (bf16[4,128,128]{2,1,0:T(8,128)(2,1)S(1)}, bf16[4,128,128]{2,1,0:T(8,128)(2,1)S(1)}, u32[]{:S(2)}, u32[]{:S(2)}) collective-permute-start(bf16[4,128,128]{2,1,0:T(8,128)(2,1)S(1)} %copy-done.29), channel_id=1, source_target_pairs={{0,160},{32,192},{64,224},{96,0},{128,32},{160,64},{192,96},{224,1... | collective-permute-start | bytes 393224 | tf_op jit(solution)/shard_map/ppermute | solution.py:202
  135.3 2.7 %collective-permute-start.24 = (bf16[2,4,144,128]{3,2,1,0:T(8,128)(2,1)}, bf16[2,4,144,128]{3,2,1,0:T(8,128)(2,1)S(1)}, u32[]{:S(2)}, u32[]{:S(2)}) collective-permute-start(bf16[2,4,144,128]{3,2,1,0:T(8,128)(2,1)} %get-tuple-element.159), channel_id=1, source_target_pairs={{0,4},{2,6},{4,0},{6,2},{1,5},{3,7},{5,1},{7,3},{8,12},{10,14},{12... | collective-permute-start | bytes 884744 | tf_op jit(solution)/shard_map/ppermute | solution.py:202
  140.7 5.5 %collective-permute-start.19 = (bf16[4,128,128]{2,1,0:T(8,128)(2,1)}, bf16[4,128,128]{2,1,0:T(8,128)(2,1)S(1)}, u32[]{:S(2)}, u32[]{:S(2)}) collective-permute-start(bf16[4,128,128]{2,1,0:T(8,128)(2,1)} %get-tuple-element.148), channel_id=1, source_target_pairs={{0,128},{32,160},{64,192},{96,224},{128,0},{160,32},{192,64},{224,... | collective-permute-start | bytes 393224 | tf_op jit(solution)/shard_map/ppermute | solution.py:202
  146.3 3.2 %collective-permute-start.20 = (bf16[4,128,128]{2,1,0:T(8,128)(2,1)S(1)}, bf16[4,128,128]{2,1,0:T(8,128)(2,1)S(1)}, u32[]{:S(2)}, u32[]{:S(2)}) collective-permute-start(bf16[4,128,128]{2,1,0:T(8,128)(2,1)S(1)} %copy-done.27), channel_id=1, source_target_pairs={{0,96},{32,128},{64,160},{96,192},{128,224},{160,0},{192,32},{224,... | collective-permute-start | bytes 393224 | tf_op jit(solution)/shard_map/ppermute | solution.py:202
  149.5 2.7 %shard_map.90 = (bf16[4,128,128]{2,1,0:T(8,128)(2,1)}, bf16[4,128,128]{2,1,0:T(8,128)(2,1)}, bf16[4,128,128]{2,1,0:T(8,128)(2,1)}) custom-call(s32[1]{0:T(128)} %bitcast.1.z_ref, bf16[4,128,128]{2,1,0:T(8,128)(2,1)} %get-tuple-element.128.refs_0_, bf16[4,128,128]{2,1,0:T(8,128)(2,1)} %copy-done.10, bf16[4,128,128]{2,1,0:T(8,128)(2,1)} %copy-done.9, ...), custom_call_target="tpu_custom_call" | custom-call | tf_op jit(solution)/shard_map/pallas_call | solution.py:39
  154.2 2.1 %collective-permute-start.16 = (bf16[4,128,128]{2,1,0:T(8,128)(2,1)}, bf16[4,128,128]{2,1,0:T(8,128)(2,1)S(1)}, u32[]{:S(2)}, u32[]{:S(2)}) collective-permute-start(bf16[4,128,128]{2,1,0:T(8,128)(2,1)} %get-tuple-element.145), channel_id=1, source_target_pairs={{0,224},{32,0},{64,32},{96,64},{128,96},{160,128},{192,160},{224,1... | collective-permute-start | bytes 393224 | tf_op jit(solution)/shard_map/ppermute | solution.py:202
  156.3 2.9 %collective-permute-done.20.refs_5_ = bf16[4,128,128]{2,1,0:T(8,128)(2,1)S(1)} collective-permute-done((bf16[4,128,128]{2,1,0:T(8,128)(2,1)S(1)}, bf16[4,128,128]{2,1,0:T(8,128)(2,1)S(1)}, u32[]{:S(2)}, u32[]{:S(2)}) %collective-permute-start.20) | collective-permute-done | bytes 131104 | tf_op jit(solution)/shard_map/ppermute | solution.py:202
  159.1 3.6 %collective-permute-start.22 = (bf16[4,128,128]{2,1,0:T(8,128)(2,1)}, bf16[4,128,128]{2,1,0:T(8,128)(2,1)S(1)}, u32[]{:S(2)}, u32[]{:S(2)}) collective-permute-start(bf16[4,128,128]{2,1,0:T(8,128)(2,1)} %get-tuple-element.156), channel_id=1, source_target_pairs={{0,32},{32,64},{64,96},{96,128},{128,160},{160,192},{192,224},{224... | collective-permute-start | bytes 393224 | tf_op jit(solution)/shard_map/ppermute | solution.py:202
  162.8 3.2 %collective-permute-done.22.refs_7_ = bf16[4,128,128]{2,1,0:T(8,128)(2,1)S(1)} collective-permute-done((bf16[4,128,128]{2,1,0:T(8,128)(2,1)}, bf16[4,128,128]{2,1,0:T(8,128)(2,1)S(1)}, u32[]{:S(2)}, u32[]{:S(2)}) %collective-permute-start.22) | collective-permute-done | bytes 131104 | tf_op jit(solution)/shard_map/ppermute | solution.py:202
  166.7 3.2 %shard_map.91 = bf16[128,4096]{1,0:T(8,128)(2,1)} custom-call(s32[1]{0:T(128)} %bitcast.me_ref, s32[1]{0:T(128)} %bitcast.1.z_ref, bf16[4,128,128]{2,1,0:T(8,128)(2,1)} %get-tuple-element.144.refs_0_, bf16[4,128,128]{2,1,0:T(8,128)(2,1)} %copy-done.21, bf16[4,128,128]{2,1,0:T(8,128)(2,1)} %copy-done.12, bf16[4,128,128]{2,1,0:T(8,128)(2,1)} %copy-done.13, ...), custom_call_target="tpu_custom_call" | custom-call | tf_op jit(solution)/shard_map/pallas_call | solution.py:39
  (106 shorter events, 35.8 us)
Async XLA Ops:
  0.0 2.9 %collective-permute-start = (bf16[8,128,512]{2,1,0:T(8,128)(2,1)}, bf16[8,128,512]{2,1,0:T(8,128)(2,1)S(1)}, u32[]{:S(2)}, u32[]{:S(2)}) collective-permute-start(bf16[8,128,512]{2,1,0:T(8,128)(2,1)} %param.12), channel_id=1, source_target_pairs={{0,1},{1,0},{2,3},{3,2},{4,5},{5,4},{6,7},{7,6},{8,9},{9,8},{10,11... | collective-permute-start | bytes 3145736 | tf_op jit(solution)/shard_map/ppermute | solution.py:202
  5.9 63.9 %all-to-all-start = ((bf16[32,272,128]{2,1,0:T(8,128)(2,1)}), bf16[32,272,128]{2,1,0:T(8,128)(2,1)S(1)}, u32[]{:S(2)}, u32[]{:S(2)}) async-start(bf16[32,272,128]{2,1,0:T(8,128)(2,1)} %shard_map.82), calls=%async_computation | async-start | bytes 4456448 | tf_op jit(solution)/shard_map/all_to_all | solution.py:222
  17.6 42.5 %copy-start.5 = (f32[4]{0:T(128)S(1)}, f32[4]{0:T(128)}, u32[]{:S(2)}) copy-start(f32[4]{0:T(128)} %gate_ref.1) | copy-start | bytes 52
  22.0 12.4 %collective-permute-start.1 = (bf16[3,128,512]{2,1,0:T(8,128)(2,1)}, bf16[3,128,512]{2,1,0:T(8,128)(2,1)}, u32[]{:S(2)}, u32[]{:S(2)}) collective-permute-start(bf16[3,128,512]{2,1,0:T(8,128)(2,1)} %get-tuple-element.84), channel_id=1, source_target_pairs={{0,1},{1,2},{2,3},{3,4},{4,5},{5,6},{6,7},{7,0},{8,9},{9,10},{10,1... | collective-permute-start | bytes 1179656 | tf_op jit(solution)/shard_map/ppermute | solution.py:202
  22.0 14.2 %collective-permute-start.2 = (bf16[3,128,512]{2,1,0:T(8,128)(2,1)}, bf16[3,128,512]{2,1,0:T(8,128)(2,1)}, u32[]{:S(2)}, u32[]{:S(2)}) collective-permute-start(bf16[3,128,512]{2,1,0:T(8,128)(2,1)} %get-tuple-element.85), channel_id=1, source_target_pairs={{0,2},{1,3},{2,4},{3,5},{4,6},{5,7},{6,0},{7,1},{8,10},{9,11},{10,... | collective-permute-start | bytes 1179656 | tf_op jit(solution)/shard_map/ppermute | solution.py:202
  23.6 28.9 %collective-permute-start.3 = (bf16[3,128,512]{2,1,0:T(8,128)(2,1)}, bf16[3,128,512]{2,1,0:T(8,128)(2,1)}, u32[]{:S(2)}, u32[]{:S(2)}) collective-permute-start(bf16[3,128,512]{2,1,0:T(8,128)(2,1)} %get-tuple-element.86), channel_id=1, source_target_pairs={{0,3},{1,4},{2,5},{3,6},{4,7},{5,0},{6,1},{7,2},{8,11},{9,12},{10,... | collective-permute-start | bytes 1179656 | tf_op jit(solution)/shard_map/ppermute | solution.py:202
  25.9 27.7 %collective-permute-start.4 = (bf16[3,128,512]{2,1,0:T(8,128)(2,1)}, bf16[3,128,512]{2,1,0:T(8,128)(2,1)}, u32[]{:S(2)}, u32[]{:S(2)}) collective-permute-start(bf16[3,128,512]{2,1,0:T(8,128)(2,1)} %get-tuple-element.87), channel_id=1, source_target_pairs={{0,4},{1,5},{2,6},{3,7},{4,0},{5,1},{6,2},{7,3},{8,12},{9,13},{10,... | collective-permute-start | bytes 1179656 | tf_op jit(solution)/shard_map/ppermute | solution.py:202
  27.7 30.4 %collective-permute-start.5 = (bf16[3,128,512]{2,1,0:T(8,128)(2,1)}, bf16[3,128,512]{2,1,0:T(8,128)(2,1)}, u32[]{:S(2)}, u32[]{:S(2)}) collective-permute-start(bf16[3,128,512]{2,1,0:T(8,128)(2,1)} %get-tuple-element.88), channel_id=1, source_target_pairs={{0,5},{1,6},{2,7},{3,0},{4,1},{5,2},{6,3},{7,4},{8,13},{9,14},{10,... | collective-permute-start | bytes 1179656 | tf_op jit(solution)/shard_map/ppermute | solution.py:202
  34.4 23.8 %collective-permute-start.6 = (bf16[3,128,512]{2,1,0:T(8,128)(2,1)}, bf16[3,128,512]{2,1,0:T(8,128)(2,1)}, u32[]{:S(2)}, u32[]{:S(2)}) collective-permute-start(bf16[3,128,512]{2,1,0:T(8,128)(2,1)} %get-tuple-element.89), channel_id=1, source_target_pairs={{0,6},{1,7},{2,0},{3,1},{4,2},{5,3},{6,4},{7,5},{8,14},{9,15},{10,... | collective-permute-start | bytes 1179656 | tf_op jit(solution)/shard_map/ppermute | solution.py:202
  36.2 23.9 %collective-permute-start.7 = (bf16[3,128,512]{2,1,0:T(8,128)(2,1)}, bf16[3,128,512]{2,1,0:T(8,128)(2,1)}, u32[]{:S(2)}, u32[]{:S(2)}) collective-permute-start(bf16[3,128,512]{2,1,0:T(8,128)(2,1)} %get-tuple-element.90), channel_id=1, source_target_pairs={{0,7},{1,0},{2,1},{3,2},{4,3},{5,4},{6,5},{7,6},{8,15},{9,8},{10,9... | collective-permute-start | bytes 1179656 | tf_op jit(solution)/shard_map/ppermute | solution.py:202
  73.6 29.5 %copy-start.24 = (bf16[4,128,128]{2,1,0:T(8,128)(2,1)S(1)}, bf16[4,128,128]{2,1,0:T(8,128)(2,1)}, u32[]{:S(2)}) copy-start(bf16[4,128,128]{2,1,0:T(8,128)(2,1)} %get-tuple-element.116) | copy-start | bytes 393220
  73.6 40.0 %all-to-all-start.1 = ((bf16[32,10,32,128]{3,2,1,0:T(8,128)(2,1)}), bf16[32,10,32,128]{3,2,1,0:T(8,128)(2,1)}, u32[]{:S(2)}, u32[]{:S(2)}) async-start(bf16[32,10,32,128]{3,2,1,0:T(8,128)(2,1)} %shard_map.86), calls=%async_computation.1 | async-start | bytes 5242880 | tf_op jit(solution)/shard_map/all_to_all | solution.py:251
  81.9 21.2 %collective-permute-start.15 = (bf16[4,4,144,128]{3,2,1,0:T(8,128)(2,1)}, bf16[4,4,144,128]{3,2,1,0:T(8,128)(2,1)S(1)}, u32[]{:S(2)}, u32[]{:S(2)}) collective-permute-start(bf16[4,4,144,128]{3,2,1,0:T(8,128)(2,1)} %get-tuple-element.123), channel_id=1, source_target_pairs={{0,1},{1,0},{2,3},{3,2},{4,5},{5,4},{6,7},{7,6},{8,9},{9,8},{10,11... | collective-permute-start | bytes 1769480 | tf_op jit(solution)/shard_map/ppermute | solution.py:202
  82.1 13.9 %collective-permute-start.10 = (bf16[4,128,128]{2,1,0:T(8,128)(2,1)S(1)}, bf16[4,128,128]{2,1,0:T(8,128)(2,1)S(1)}, u32[]{:S(2)}, u32[]{:S(2)}) collective-permute-start(bf16[4,128,128]{2,1,0:T(8,128)(2,1)S(1)} %copy-done.28), channel_id=1, source_target_pairs={{0,96},{32,128},{64,160},{96,192},{128,224},{160,0},{192,32},{224,... | collective-permute-start | bytes 393224 | tf_op jit(solution)/shard_map/ppermute | solution.py:202
  85.4 14.5 %collective-permute-start.11 = (bf16[4,128,128]{2,1,0:T(8,128)(2,1)S(1)}, bf16[4,128,128]{2,1,0:T(8,128)(2,1)S(1)}, u32[]{:S(2)}, u32[]{:S(2)}) collective-permute-start(bf16[4,128,128]{2,1,0:T(8,128)(2,1)S(1)} %copy-done.26), channel_id=1, source_target_pairs={{0,128},{32,160},{64,192},{96,224},{128,0},{160,32},{192,64},{224,... | collective-permute-start | bytes 393224 | tf_op jit(solution)/shard_map/ppermute | solution.py:202
  88.1 20.1 %collective-permute-start.12 = (bf16[4,128,128]{2,1,0:T(8,128)(2,1)}, bf16[4,128,128]{2,1,0:T(8,128)(2,1)S(1)}, u32[]{:S(2)}, u32[]{:S(2)}) collective-permute-start(bf16[4,128,128]{2,1,0:T(8,128)(2,1)} %get-tuple-element.119), channel_id=1, source_target_pairs={{0,160},{32,192},{64,224},{96,0},{128,32},{160,64},{192,96},{224,1... | collective-permute-start | bytes 393224 | tf_op jit(solution)/shard_map/ppermute | solution.py:202
  92.5 18.3 %collective-permute-start.13 = (bf16[4,128,128]{2,1,0:T(8,128)(2,1)}, bf16[4,128,128]{2,1,0:T(8,128)(2,1)S(1)}, u32[]{:S(2)}, u32[]{:S(2)}) collective-permute-start(bf16[4,128,128]{2,1,0:T(8,128)(2,1)} %get-tuple-element.120), channel_id=1, source_target_pairs={{0,192},{32,224},{64,0},{96,32},{128,64},{160,96},{192,128},{224,1... | collective-permute-start | bytes 393224 | tf_op jit(solution)/shard_map/ppermute | solution.py:202
  96.0 15.8 %collective-permute-start.14 = (bf16[4,128,128]{2,1,0:T(8,128)(2,1)}, bf16[4,128,128]{2,1,0:T(8,128)(2,1)S(1)}, u32[]{:S(2)}, u32[]{:S(2)}) collective-permute-start(bf16[4,128,128]{2,1,0:T(8,128)(2,1)} %get-tuple-element.121), channel_id=1, source_target_pairs={{0,224},{32,0},{64,32},{96,64},{128,96},{160,128},{192,160},{224,1... | collective-permute-start | bytes 393224 | tf_op jit(solution)/shard_map/ppermute | solution.py:202
  99.9 11.8 %collective-permute-start.8 = (bf16[4,128,128]{2,1,0:T(8,128)(2,1)S(1)}, bf16[4,128,128]{2,1,0:T(8,128)(2,1)S(1)}, u32[]{:S(2)}, u32[]{:S(2)}) collective-permute-start(bf16[4,128,128]{2,1,0:T(8,128)(2,1)S(1)} %copy-done.25), channel_id=1, source_target_pairs={{0,32},{32,64},{64,96},{96,128},{128,160},{160,192},{192,224},{224... | collective-permute-start | bytes 393224 | tf_op jit(solution)/shard_map/ppermute | solution.py:202
  103.1 9.8 %collective-permute-start.9 = (bf16[4,128,128]{2,1,0:T(8,128)(2,1)S(1)}, bf16[4,128,128]{2,1,0:T(8,128)(2,1)S(1)}, u32[]{:S(2)}, u32[]{:S(2)}) collective-permute-start(bf16[4,128,128]{2,1,0:T(8,128)(2,1)S(1)} %copy-done.24), channel_id=1, source_target_pairs={{0,64},{32,96},{64,128},{96,160},{128,192},{160,224},{192,0},{224,... | collective-permute-start | bytes 393224 | tf_op jit(solution)/shard_map/ppermute | solution.py:202
  117.7 31.8 %all-to-all-start.2 = ((bf16[32,6,32,128]{3,2,1,0:T(8,128)(2,1)}), bf16[32,6,32,128]{3,2,1,0:T(8,128)(2,1)S(1)}, u32[]{:S(2)}, u32[]{:S(2)}) async-start(bf16[32,6,32,128]{3,2,1,0:T(8,128)(2,1)} %shard_map.87), calls=%async_computation.2 | async-start | bytes 3145728 | tf_op jit(solution)/shard_map/all_to_all | solution.py:251
  125.2 8.6 %collective-permute-start.21 = (bf16[4,128,128]{2,1,0:T(8,128)(2,1)S(1)}, bf16[4,128,128]{2,1,0:T(8,128)(2,1)S(1)}, u32[]{:S(2)}, u32[]{:S(2)}) collective-permute-start(bf16[4,128,128]{2,1,0:T(8,128)(2,1)S(1)} %copy-done.31), channel_id=1, source_target_pairs={{0,64},{32,96},{64,128},{96,160},{128,192},{160,224},{192,0},{224,... | collective-permute-start | bytes 393224 | tf_op jit(solution)/shard_map/ppermute | solution.py:202
  127.2 13.6 %collective-permute-start.17 = (bf16[4,128,128]{2,1,0:T(8,128)(2,1)S(1)}, bf16[4,128,128]{2,1,0:T(8,128)(2,1)S(1)}, u32[]{:S(2)}, u32[]{:S(2)}) collective-permute-start(bf16[4,128,128]{2,1,0:T(8,128)(2,1)S(1)} %copy-done.30), channel_id=1, source_target_pairs={{0,192},{32,224},{64,0},{96,32},{128,64},{160,96},{192,128},{224,1... | collective-permute-start | bytes 393224 | tf_op jit(solution)/shard_map/ppermute | solution.py:202
  129.4 16.9 %collective-permute-start.18 = (bf16[4,128,128]{2,1,0:T(8,128)(2,1)S(1)}, bf16[4,128,128]{2,1,0:T(8,128)(2,1)S(1)}, u32[]{:S(2)}, u32[]{:S(2)}) collective-permute-start(bf16[4,128,128]{2,1,0:T(8,128)(2,1)S(1)} %copy-done.29), channel_id=1, source_target_pairs={{0,160},{32,192},{64,224},{96,0},{128,32},{160,64},{192,96},{224,1... | collective-permute-start | bytes 393224 | tf_op jit(solution)/shard_map/ppermute | solution.py:202
  133.8 32.2 %copy-start.11 = (bf16[4,128,128]{2,1,0:T(8,128)(2,1)}, bf16[4,128,128]{2,1,0:T(8,128)(2,1)S(1)}, u32[]{:S(2)}) copy-start(bf16[4,128,128]{2,1,0:T(8,128)(2,1)S(1)} %collective-permute-done.21.refs_6_) | copy-start | bytes 393220
  133.8 28.9 %collective-permute-start.23 = (bf16[2,4,144,128]{3,2,1,0:T(8,128)(2,1)}, bf16[2,4,144,128]{3,2,1,0:T(8,128)(2,1)S(1)}, u32[]{:S(2)}, u32[]{:S(2)}) collective-permute-start(bf16[2,4,144,128]{3,2,1,0:T(8,128)(2,1)} %get-tuple-element.158), channel_id=1, source_target_pairs={{0,2},{2,4},{4,6},{6,0},{1,3},{3,5},{5,7},{7,1},{8,10},{10,12},{12... | collective-permute-start | bytes 884744 | tf_op jit(solution)/shard_map/ppermute | solution.py:202
  135.3 27.5 %collective-permute-start.24 = (bf16[2,4,144,128]{3,2,1,0:T(8,128)(2,1)}, bf16[2,4,144,128]{3,2,1,0:T(8,128)(2,1)S(1)}, u32[]{:S(2)}, u32[]{:S(2)}) collective-permute-start(bf16[2,4,144,128]{3,2,1,0:T(8,128)(2,1)} %get-tuple-element.159), channel_id=1, source_target_pairs={{0,4},{2,6},{4,0},{6,2},{1,5},{3,7},{5,1},{7,3},{8,12},{10,14},{12... | collective-permute-start | bytes 884744 | tf_op jit(solution)/shard_map/ppermute | solution.py:202
  138.0 24.8 %collective-permute-start.25 = (bf16[2,4,144,128]{3,2,1,0:T(8,128)(2,1)S(1)}, bf16[2,4,144,128]{3,2,1,0:T(8,128)(2,1)S(1)}, u32[]{:S(2)}, u32[]{:S(2)}) collective-permute-start(bf16[2,4,144,128]{3,2,1,0:T(8,128)(2,1)S(1)} %copy-done.23), channel_id=1, source_target_pairs={{0,6},{2,0},{4,2},{6,4},{1,7},{3,1},{5,3},{7,5},{8,14},{10,8},{12,... | collective-permute-start | bytes 884744 | tf_op jit(solution)/shard_map/ppermute | solution.py:202
  140.7 13.4 %collective-permute-start.19 = (bf16[4,128,128]{2,1,0:T(8,128)(2,1)}, bf16[4,128,128]{2,1,0:T(8,128)(2,1)S(1)}, u32[]{:S(2)}, u32[]{:S(2)}) collective-permute-start(bf16[4,128,128]{2,1,0:T(8,128)(2,1)} %get-tuple-element.148), channel_id=1, source_target_pairs={{0,128},{32,160},{64,192},{96,224},{128,0},{160,32},{192,64},{224,... | collective-permute-start | bytes 393224 | tf_op jit(solution)/shard_map/ppermute | solution.py:202
  146.3 12.9 %collective-permute-start.20 = (bf16[4,128,128]{2,1,0:T(8,128)(2,1)S(1)}, bf16[4,128,128]{2,1,0:T(8,128)(2,1)S(1)}, u32[]{:S(2)}, u32[]{:S(2)}) collective-permute-start(bf16[4,128,128]{2,1,0:T(8,128)(2,1)S(1)} %copy-done.27), channel_id=1, source_target_pairs={{0,96},{32,128},{64,160},{96,192},{128,224},{160,0},{192,32},{224,... | collective-permute-start | bytes 393224 | tf_op jit(solution)/shard_map/ppermute | solution.py:202
  154.2 8.6 %collective-permute-start.16 = (bf16[4,128,128]{2,1,0:T(8,128)(2,1)}, bf16[4,128,128]{2,1,0:T(8,128)(2,1)S(1)}, u32[]{:S(2)}, u32[]{:S(2)}) collective-permute-start(bf16[4,128,128]{2,1,0:T(8,128)(2,1)} %get-tuple-element.145), channel_id=1, source_target_pairs={{0,224},{32,0},{64,32},{96,64},{128,96},{160,128},{192,160},{224,1... | collective-permute-start | bytes 393224 | tf_op jit(solution)/shard_map/ppermute | solution.py:202
  159.1 6.8 %collective-permute-start.22 = (bf16[4,128,128]{2,1,0:T(8,128)(2,1)}, bf16[4,128,128]{2,1,0:T(8,128)(2,1)S(1)}, u32[]{:S(2)}, u32[]{:S(2)}) collective-permute-start(bf16[4,128,128]{2,1,0:T(8,128)(2,1)} %get-tuple-element.156), channel_id=1, source_target_pairs={{0,32},{32,64},{64,96},{96,128},{128,160},{160,192},{192,224},{224... | collective-permute-start | bytes 393224 | tf_op jit(solution)/shard_map/ppermute | solution.py:202
  (29 other events, 283.8 us)

commit v4 on v3

--- a/solution.py
+++ b/solution.py
@@ -70,17 +70,20 @@
 
 
 def gather_kernel(shifts, z_ref, ids_ref, table_ref, out_ref):
-    def one(dest, carry):
+    start = pl.program_id(0) * out_ref.shape[0]
+
+    def one(row, carry):
+        dest = start + row
         for i, shift in enumerate(shifts):
             plane = (z_ref[0] + PLANES - shift) & (PLANES - 1)
             for k in range(2):
                 block = ids_ref[plane * 2 * PLANE_DEVS + 2 * dest + k]
                 first = pl.multiple_of((block & (SLOTS - 1)) * ROWS, ROWS)
                 owner = lax.shift_right_logical(block, 3)
-                out_ref[dest, 2 * i + k] = table_ref[owner, pl.ds(first, ROWS), :]
+                out_ref[row, 2 * i + k] = table_ref[owner, pl.ds(first, ROWS), :]
         return carry
 
-    lax.fori_loop(0, PLANE_DEVS, one, 0, unroll=4)
+    lax.fori_loop(0, out_ref.shape[0], one, 0, unroll=4)
 
 
 def query_kernel(z_ref, q_ref, *out_refs):
@@ -240,12 +243,16 @@
     all_ids = table[:, SLOTS * ROWS :, 0].astype(jnp.int32).reshape(MEM_DEVS * TAIL)
 
     def gathered(shifts, table):
-        return call(
+        shape = (PLANE_DEVS, 2 * len(shifts), ROWS, DH)
+        smem = pl.BlockSpec(memory_space=pltpu.SMEM)
+        return pl.pallas_call(
             functools.partial(gather_kernel, shifts),
-            [(PLANE_DEVS, 2 * len(shifts), ROWS, DH)],
-            [z, all_ids],
-            [table],
-        )[0]
+            out_shape=pltpu.HBM(shape, jnp.bfloat16),
+            grid=(4,),
+            in_specs=[smem, smem, whole(table)],
+            out_specs=pl.BlockSpec((PLANE_DEVS // 4, *shape[1:]), lambda i: (i, 0, 0, 0)),
+            compiler_params=pltpu.CompilerParams(vmem_limit_bytes=12 * 1024 * 1024),
+        )(z, all_ids, table)
 
     def fetch(requested):
         fetched = lax.all_to_all(

time: 170 us -> 170 us (level)
    pallas_call x0 -> x2, Pallas kernels: none -> 5.62 us  [gathered(): pl.pallas_call(functools.partial(gather_kernel, shifts), out_shape=pltpu....]
    pallas_call x10 -> x8, Pallas kernels: 30.8 us -> 25.4 us  [call(): pl.pallas_call(kernel, out_shape=outs, grid=(1,), in_specs=[pl.BlockSpec(...]
where the time goes in v4:
time: 170 us
  starting transfers between devices  91.7 us (54%)
  waiting for transfers between devices  40.8 us (24%)
  Pallas kernels  31 us (18%)
  local copies, waits for them, and re-layouts  4.72 us (3%)
    ppermute x26, starting transfers between devices, shifted(): lax.ppermute(array, axis, [(i, (i + shift) % size) for i in range(size)])  64.3 us
    ppermute x26, waiting for transfers between devices, shifted(): lax.ppermute(array, axis, [(i, (i + shift) % size) for i in range(size)])  39.8 us
    pallas_call x8, Pallas kernels, call(): pl.pallas_call(kernel, out_shape=outs, grid=(1,), in_specs=[pl.BlockSpec(...  25.4 us
    all_to_all x2, starting transfers between devices, fetch(): lax.all_to_all(requested, ('x', 'y', 'c'), split_axis=0, concat_axis=0, t...  15.7 us
    all_to_all x1, starting transfers between devices, on_device(): lax.all_to_all(spread, ('z', 'x'), split_axis=0, concat_axis=0, tiled=True)  11.7 us
    pallas_call x2, Pallas kernels, gathered(): pl.pallas_call(functools.partial(gather_kernel, shifts), out_shape=pltpu....  5.62 us
    unnamed x64, local copies, waits for them, and re-layouts  4.39 us
  transfers between devices with their start and end apart: 29, of which 17 were waited for; matrix products, arithmetic and copies ran while one was open for 1% of the time, Pallas kernels for 11%

profile of v4, /device:TPU:6, one launch (start us, length us, event | category | flops | bytes accessed | tf_op | source)
XLA Modules:
  0.0 169.8 jit_solution(4372699665183045225)
XLA Ops:
  0.9 2.0 %collective-permute-done.swapped_ref = bf16[8,128,512]{2,1,0:T(8,128)(2,1)S(1)} collective-permute-done((bf16[8,128,512]{2,1,0:T(8,128)(2,1)}, bf16[8,128,512]{2,1,0:T(8,128)(2,1)S(1)}, u32[]{:S(2)}, u32[]{:S(2)}) %collective-permute-start) | collective-permute-done | bytes 1048608 | tf_op jit(solution)/shard_map/ppermute | solution.py:205
  5.9 11.7 %all-to-all-start = ((bf16[32,272,128]{2,1,0:T(8,128)(2,1)}), bf16[32,272,128]{2,1,0:T(8,128)(2,1)S(1)}, u32[]{:S(2)}, u32[]{:S(2)}) async-start(bf16[32,272,128]{2,1,0:T(8,128)(2,1)} %shard_map.82), calls=%async_computation | async-start | bytes 4456448 | tf_op jit(solution)/shard_map/all_to_all | solution.py:225
  23.6 2.3 %collective-permute-start.3 = (bf16[3,128,512]{2,1,0:T(8,128)(2,1)}, bf16[3,128,512]{2,1,0:T(8,128)(2,1)}, u32[]{:S(2)}, u32[]{:S(2)}) collective-permute-start(bf16[3,128,512]{2,1,0:T(8,128)(2,1)} %get-tuple-element.86), channel_id=1, source_target_pairs={{0,3},{1,4},{2,5},{3,6},{4,7},{5,0},{6,1},{7,2},{8,11},{9,12},{10,... | collective-permute-start | bytes 1179656 | tf_op jit(solution)/shard_map/ppermute | solution.py:205
  29.5 4.9 %collective-permute-done.1.refs_1_ = bf16[3,128,512]{2,1,0:T(8,128)(2,1)} collective-permute-done((bf16[3,128,512]{2,1,0:T(8,128)(2,1)}, bf16[3,128,512]{2,1,0:T(8,128)(2,1)}, u32[]{:S(2)}, u32[]{:S(2)}) %collective-permute-start.1) | collective-permute-done | bytes 393248 | tf_op jit(solution)/shard_map/ppermute | solution.py:205
  36.2 8.1 %collective-permute-start.7 = (bf16[3,128,512]{2,1,0:T(8,128)(2,1)}, bf16[3,128,512]{2,1,0:T(8,128)(2,1)}, u32[]{:S(2)}, u32[]{:S(2)}) collective-permute-start(bf16[3,128,512]{2,1,0:T(8,128)(2,1)} %get-tuple-element.90), channel_id=1, source_target_pairs={{0,7},{1,0},{2,1},{3,2},{4,3},{5,4},{6,5},{7,6},{8,15},{9,8},{10,9... | collective-permute-start | bytes 1179656 | tf_op jit(solution)/shard_map/ppermute | solution.py:205
  45.7 6.8 %collective-permute-done.3.refs_3_ = bf16[3,128,512]{2,1,0:T(8,128)(2,1)} collective-permute-done((bf16[3,128,512]{2,1,0:T(8,128)(2,1)}, bf16[3,128,512]{2,1,0:T(8,128)(2,1)}, u32[]{:S(2)}, u32[]{:S(2)}) %collective-permute-start.3) | collective-permute-done | bytes 393248 | tf_op jit(solution)/shard_map/ppermute | solution.py:205
  53.6 4.6 %collective-permute-done.5.refs_5_ = bf16[3,128,512]{2,1,0:T(8,128)(2,1)} collective-permute-done((bf16[3,128,512]{2,1,0:T(8,128)(2,1)}, bf16[3,128,512]{2,1,0:T(8,128)(2,1)}, u32[]{:S(2)}, u32[]{:S(2)}) %collective-permute-start.5) | collective-permute-done | bytes 393248 | tf_op jit(solution)/shard_map/ppermute | solution.py:205
  60.1 9.5 %shard_map.84 = (bf16[4,4,144,128]{3,2,1,0:T(8,128)(2,1)}, bf16[4,4,144,128]{3,2,1,0:T(8,128)(2,1)}) custom-call(s32[1]{0:T(128)} %bitcast.me_ref, f32[4]{0:T(128)S(1)} %copy-done.5, bf16[3,128,512]{2,1,0:T(8,128)(2,1)} %get-tuple-element.83.refs_0_, bf16[3,128,512]{2,1,0:T(8,128)(2,1)} %collective-permute-done.1.refs_1_, ...), custom_call_target="tpu_custom_call" | custom-call | tf_op jit(solution)/shard_map/pallas_call | solution.py:39
  70.5 3.1 %shard_map.86 = bf16[32,10,32,128]{3,2,1,0:T(8,128)(2,1)} custom-call(s32[1]{0:T(128)} %bitcast.1.z_ref, s32[512]{0:T(512)S(1)} %reshape.33.ids_ref, bf16[32,272,128]{2,1,0:T(8,128)(2,1)S(1)} %all-to-all-done.table_ref), custom_call_target="tpu_custom_call" | custom-call | tf_op jit(solution)/shard_map/pallas_call | solution.py:248
  73.6 8.2 %all-to-all-start.1 = ((bf16[32,10,32,128]{3,2,1,0:T(8,128)(2,1)}), bf16[32,10,32,128]{3,2,1,0:T(8,128)(2,1)}, u32[]{:S(2)}, u32[]{:S(2)}) async-start(bf16[32,10,32,128]{3,2,1,0:T(8,128)(2,1)} %shard_map.86), calls=%async_computation.1 | async-start | bytes 5242880 | tf_op jit(solution)/shard_map/all_to_all | solution.py:258
  82.1 3.3 %collective-permute-start.10 = (bf16[4,128,128]{2,1,0:T(8,128)(2,1)S(1)}, bf16[4,128,128]{2,1,0:T(8,128)(2,1)S(1)}, u32[]{:S(2)}, u32[]{:S(2)}) collective-permute-start(bf16[4,128,128]{2,1,0:T(8,128)(2,1)S(1)} %copy-done.28), channel_id=1, source_target_pairs={{0,96},{32,128},{64,160},{96,192},{128,224},{160,0},{192,32},{224,... | collective-permute-start | bytes 393224 | tf_op jit(solution)/shard_map/ppermute | solution.py:205
  85.4 2.7 %collective-permute-start.11 = (bf16[4,128,128]{2,1,0:T(8,128)(2,1)S(1)}, bf16[4,128,128]{2,1,0:T(8,128)(2,1)S(1)}, u32[]{:S(2)}, u32[]{:S(2)}) collective-permute-start(bf16[4,128,128]{2,1,0:T(8,128)(2,1)S(1)} %copy-done.26), channel_id=1, source_target_pairs={{0,128},{32,160},{64,192},{96,224},{128,0},{160,32},{192,64},{224,... | collective-permute-start | bytes 393224 | tf_op jit(solution)/shard_map/ppermute | solution.py:205
  88.1 4.4 %collective-permute-start.12 = (bf16[4,128,128]{2,1,0:T(8,128)(2,1)}, bf16[4,128,128]{2,1,0:T(8,128)(2,1)S(1)}, u32[]{:S(2)}, u32[]{:S(2)}) collective-permute-start(bf16[4,128,128]{2,1,0:T(8,128)(2,1)} %get-tuple-element.119), channel_id=1, source_target_pairs={{0,160},{32,192},{64,224},{96,0},{128,32},{160,64},{192,96},{224,1... | collective-permute-start | bytes 393224 | tf_op jit(solution)/shard_map/ppermute | solution.py:205
  93.1 2.9 %collective-permute-done.10.refs_1_ = bf16[4,128,128]{2,1,0:T(8,128)(2,1)S(1)} collective-permute-done((bf16[4,128,128]{2,1,0:T(8,128)(2,1)S(1)}, bf16[4,128,128]{2,1,0:T(8,128)(2,1)S(1)}, u32[]{:S(2)}, u32[]{:S(2)}) %collective-permute-start.10) | collective-permute-done | bytes 131104 | tf_op jit(solution)/shard_map/ppermute | solution.py:205
  96.0 2.2 %collective-permute-start.14 = (bf16[4,128,128]{2,1,0:T(8,128)(2,1)}, bf16[4,128,128]{2,1,0:T(8,128)(2,1)S(1)}, u32[]{:S(2)}, u32[]{:S(2)}) collective-permute-start(bf16[4,128,128]{2,1,0:T(8,128)(2,1)} %get-tuple-element.121), channel_id=1, source_target_pairs={{0,224},{32,0},{64,32},{96,64},{128,96},{160,128},{192,160},{224,1... | collective-permute-start | bytes 393224 | tf_op jit(solution)/shard_map/ppermute | solution.py:205
  99.9 3.1 %collective-permute-start.8 = (bf16[4,128,128]{2,1,0:T(8,128)(2,1)S(1)}, bf16[4,128,128]{2,1,0:T(8,128)(2,1)S(1)}, u32[]{:S(2)}, u32[]{:S(2)}) collective-permute-start(bf16[4,128,128]{2,1,0:T(8,128)(2,1)S(1)} %copy-done.25), channel_id=1, source_target_pairs={{0,32},{32,64},{64,96},{96,128},{128,160},{160,192},{192,224},{224... | collective-permute-start | bytes 393224 | tf_op jit(solution)/shard_map/ppermute | solution.py:205
  104.8 2.6 %shard_map.87 = bf16[32,6,32,128]{3,2,1,0:T(8,128)(2,1)} custom-call(s32[1]{0:T(128)} %bitcast.1.z_ref, s32[512]{0:T(512)S(1)} %reshape.33.ids_ref, bf16[32,272,128]{2,1,0:T(8,128)(2,1)S(1)} %all-to-all-done.table_ref), custom_call_target="tpu_custom_call" | custom-call | tf_op jit(solution)/shard_map/pallas_call | solution.py:248
  108.5 2.4 %collective-permute-done.13.refs_4_ = bf16[4,128,128]{2,1,0:T(8,128)(2,1)S(1)} collective-permute-done((bf16[4,128,128]{2,1,0:T(8,128)(2,1)}, bf16[4,128,128]{2,1,0:T(8,128)(2,1)S(1)}, u32[]{:S(2)}, u32[]{:S(2)}) %collective-permute-start.13) | collective-permute-done | bytes 131104 | tf_op jit(solution)/shard_map/ppermute | solution.py:205
  113.6 4.0 %shard_map.89 = (bf16[4,128,128]{2,1,0:T(8,128)(2,1)}, bf16[4,128,128]{2,1,0:T(8,128)(2,1)}, bf16[4,128,128]{2,1,0:T(8,128)(2,1)}, bf16[4,128,128]{2,1,0:T(8,128)(2,1)}, bf16[4,128,128]{2,1,0:T(8,128)(2,1)}) custom-call(s32[1]{0:T(128)} %bitcast.1.z_ref, bf16[4,128,128]{2,1,0:T(8,128)(2,1)} %copy-done.15, bf16[4,128,128]{2,1,0:T(8,128)(2,1)} %copy-done.14, ...), custom_call_target="tpu_custom_call" | custom-call | tf_op jit(solution)/shard_map/pallas_call | solution.py:39
  117.7 7.4 %all-to-all-start.2 = ((bf16[32,6,32,128]{3,2,1,0:T(8,128)(2,1)}), bf16[32,6,32,128]{3,2,1,0:T(8,128)(2,1)S(1)}, u32[]{:S(2)}, u32[]{:S(2)}) async-start(bf16[32,6,32,128]{3,2,1,0:T(8,128)(2,1)} %shard_map.87), calls=%async_computation.2 | async-start | bytes 3145728 | tf_op jit(solution)/shard_map/all_to_all | solution.py:258
  125.1 2.0 %collective-permute-start.21 = (bf16[4,128,128]{2,1,0:T(8,128)(2,1)S(1)}, bf16[4,128,128]{2,1,0:T(8,128)(2,1)S(1)}, u32[]{:S(2)}, u32[]{:S(2)}) collective-permute-start(bf16[4,128,128]{2,1,0:T(8,128)(2,1)S(1)} %copy-done.31), channel_id=1, source_target_pairs={{0,64},{32,96},{64,128},{96,160},{128,192},{160,224},{192,0},{224,... | collective-permute-start | bytes 393224 | tf_op jit(solution)/shard_map/ppermute | solution.py:205
  127.2 2.2 %collective-permute-start.17 = (bf16[4,128,128]{2,1,0:T(8,128)(2,1)S(1)}, bf16[4,128,128]{2,1,0:T(8,128)(2,1)S(1)}, u32[]{:S(2)}, u32[]{:S(2)}) collective-permute-start(bf16[4,128,128]{2,1,0:T(8,128)(2,1)S(1)} %copy-done.30), channel_id=1, source_target_pairs={{0,192},{32,224},{64,0},{96,32},{128,64},{160,96},{192,128},{224,1... | collective-permute-start | bytes 393224 | tf_op jit(solution)/shard_map/ppermute | solution.py:205
  129.4 4.4 %collective-permute-start.18 = (bf16[4,128,128]{2,1,0:T(8,128)(2,1)S(1)}, bf16[4,128,128]{2,1,0:T(8,128)(2,1)S(1)}, u32[]{:S(2)}, u32[]{:S(2)}) collective-permute-start(bf16[4,128,128]{2,1,0:T(8,128)(2,1)S(1)} %copy-done.29), channel_id=1, source_target_pairs={{0,160},{32,192},{64,224},{96,0},{128,32},{160,64},{192,96},{224,1... | collective-permute-start | bytes 393224 | tf_op jit(solution)/shard_map/ppermute | solution.py:205
  135.3 2.7 %collective-permute-start.24 = (bf16[2,4,144,128]{3,2,1,0:T(8,128)(2,1)}, bf16[2,4,144,128]{3,2,1,0:T(8,128)(2,1)S(1)}, u32[]{:S(2)}, u32[]{:S(2)}) collective-permute-start(bf16[2,4,144,128]{3,2,1,0:T(8,128)(2,1)} %get-tuple-element.159), channel_id=1, source_target_pairs={{0,4},{2,6},{4,0},{6,2},{1,5},{3,7},{5,1},{7,3},{8,12},{10,14},{12... | collective-permute-start | bytes 884744 | tf_op jit(solution)/shard_map/ppermute | solution.py:205
  140.7 5.5 %collective-permute-start.19 = (bf16[4,128,128]{2,1,0:T(8,128)(2,1)}, bf16[4,128,128]{2,1,0:T(8,128)(2,1)S(1)}, u32[]{:S(2)}, u32[]{:S(2)}) collective-permute-start(bf16[4,128,128]{2,1,0:T(8,128)(2,1)} %get-tuple-element.148), channel_id=1, source_target_pairs={{0,128},{32,160},{64,192},{96,224},{128,0},{160,32},{192,64},{224,... | collective-permute-start | bytes 393224 | tf_op jit(solution)/shard_map/ppermute | solution.py:205
  146.3 3.2 %collective-permute-start.20 = (bf16[4,128,128]{2,1,0:T(8,128)(2,1)S(1)}, bf16[4,128,128]{2,1,0:T(8,128)(2,1)S(1)}, u32[]{:S(2)}, u32[]{:S(2)}) collective-permute-start(bf16[4,128,128]{2,1,0:T(8,128)(2,1)S(1)} %copy-done.27), channel_id=1, source_target_pairs={{0,96},{32,128},{64,160},{96,192},{128,224},{160,0},{192,32},{224,... | collective-permute-start | bytes 393224 | tf_op jit(solution)/shard_map/ppermute | solution.py:205
  149.5 2.7 %shard_map.90 = (bf16[4,128,128]{2,1,0:T(8,128)(2,1)}, bf16[4,128,128]{2,1,0:T(8,128)(2,1)}, bf16[4,128,128]{2,1,0:T(8,128)(2,1)}) custom-call(s32[1]{0:T(128)} %bitcast.1.z_ref, bf16[4,128,128]{2,1,0:T(8,128)(2,1)} %get-tuple-element.128.refs_0_, bf16[4,128,128]{2,1,0:T(8,128)(2,1)} %copy-done.10, bf16[4,128,128]{2,1,0:T(8,128)(2,1)} %copy-done.9, ...), custom_call_target="tpu_custom_call" | custom-call | tf_op jit(solution)/shard_map/pallas_call | solution.py:39
  154.1 2.1 %collective-permute-start.16 = (bf16[4,128,128]{2,1,0:T(8,128)(2,1)}, bf16[4,128,128]{2,1,0:T(8,128)(2,1)S(1)}, u32[]{:S(2)}, u32[]{:S(2)}) collective-permute-start(bf16[4,128,128]{2,1,0:T(8,128)(2,1)} %get-tuple-element.145), channel_id=1, source_target_pairs={{0,224},{32,0},{64,32},{96,64},{128,96},{160,128},{192,160},{224,1... | collective-permute-start | bytes 393224 | tf_op jit(solution)/shard_map/ppermute | solution.py:205
  156.2 2.9 %collective-permute-done.20.refs_5_ = bf16[4,128,128]{2,1,0:T(8,128)(2,1)S(1)} collective-permute-done((bf16[4,128,128]{2,1,0:T(8,128)(2,1)S(1)}, bf16[4,128,128]{2,1,0:T(8,128)(2,1)S(1)}, u32[]{:S(2)}, u32[]{:S(2)}) %collective-permute-start.20) | collective-permute-done | bytes 131104 | tf_op jit(solution)/shard_map/ppermute | solution.py:205
  159.1 3.6 %collective-permute-start.22 = (bf16[4,128,128]{2,1,0:T(8,128)(2,1)}, bf16[4,128,128]{2,1,0:T(8,128)(2,1)S(1)}, u32[]{:S(2)}, u32[]{:S(2)}) collective-permute-start(bf16[4,128,128]{2,1,0:T(8,128)(2,1)} %get-tuple-element.156), channel_id=1, source_target_pairs={{0,32},{32,64},{64,96},{96,128},{128,160},{160,192},{192,224},{224... | collective-permute-start | bytes 393224 | tf_op jit(solution)/shard_map/ppermute | solution.py:205
  162.8 3.2 %collective-permute-done.22.refs_7_ = bf16[4,128,128]{2,1,0:T(8,128)(2,1)S(1)} collective-permute-done((bf16[4,128,128]{2,1,0:T(8,128)(2,1)}, bf16[4,128,128]{2,1,0:T(8,128)(2,1)S(1)}, u32[]{:S(2)}, u32[]{:S(2)}) %collective-permute-start.22) | collective-permute-done | bytes 131104 | tf_op jit(solution)/shard_map/ppermute | solution.py:205
  166.6 3.2 %shard_map.91 = bf16[128,4096]{1,0:T(8,128)(2,1)} custom-call(s32[1]{0:T(128)} %bitcast.me_ref, s32[1]{0:T(128)} %bitcast.1.z_ref, bf16[4,128,128]{2,1,0:T(8,128)(2,1)} %get-tuple-element.144.refs_0_, bf16[4,128,128]{2,1,0:T(8,128)(2,1)} %copy-done.21, bf16[4,128,128]{2,1,0:T(8,128)(2,1)} %copy-done.12, bf16[4,128,128]{2,1,0:T(8,128)(2,1)} %copy-done.13, ...), custom_call_target="tpu_custom_call" | custom-call | tf_op jit(solution)/shard_map/pallas_call | solution.py:39
  (106 shorter events, 35.8 us)
Async XLA Ops:
  0.0 2.9 %collective-permute-start = (bf16[8,128,512]{2,1,0:T(8,128)(2,1)}, bf16[8,128,512]{2,1,0:T(8,128)(2,1)S(1)}, u32[]{:S(2)}, u32[]{:S(2)}) collective-permute-start(bf16[8,128,512]{2,1,0:T(8,128)(2,1)} %param.12), channel_id=1, source_target_pairs={{0,1},{1,0},{2,3},{3,2},{4,5},{5,4},{6,7},{7,6},{8,9},{9,8},{10,11... | collective-permute-start | bytes 3145736 | tf_op jit(solution)/shard_map/ppermute | solution.py:205
  5.9 63.9 %all-to-all-start = ((bf16[32,272,128]{2,1,0:T(8,128)(2,1)}), bf16[32,272,128]{2,1,0:T(8,128)(2,1)S(1)}, u32[]{:S(2)}, u32[]{:S(2)}) async-start(bf16[32,272,128]{2,1,0:T(8,128)(2,1)} %shard_map.82), calls=%async_computation | async-start | bytes 4456448 | tf_op jit(solution)/shard_map/all_to_all | solution.py:225
  17.6 42.5 %copy-start.5 = (f32[4]{0:T(128)S(1)}, f32[4]{0:T(128)}, u32[]{:S(2)}) copy-start(f32[4]{0:T(128)} %gate_ref.1) | copy-start | bytes 52
  22.0 12.4 %collective-permute-start.1 = (bf16[3,128,512]{2,1,0:T(8,128)(2,1)}, bf16[3,128,512]{2,1,0:T(8,128)(2,1)}, u32[]{:S(2)}, u32[]{:S(2)}) collective-permute-start(bf16[3,128,512]{2,1,0:T(8,128)(2,1)} %get-tuple-element.84), channel_id=1, source_target_pairs={{0,1},{1,2},{2,3},{3,4},{4,5},{5,6},{6,7},{7,0},{8,9},{9,10},{10,1... | collective-permute-start | bytes 1179656 | tf_op jit(solution)/shard_map/ppermute | solution.py:205
  22.0 14.2 %collective-permute-start.2 = (bf16[3,128,512]{2,1,0:T(8,128)(2,1)}, bf16[3,128,512]{2,1,0:T(8,128)(2,1)}, u32[]{:S(2)}, u32[]{:S(2)}) collective-permute-start(bf16[3,128,512]{2,1,0:T(8,128)(2,1)} %get-tuple-element.85), channel_id=1, source_target_pairs={{0,2},{1,3},{2,4},{3,5},{4,6},{5,7},{6,0},{7,1},{8,10},{9,11},{10,... | collective-permute-start | bytes 1179656 | tf_op jit(solution)/shard_map/ppermute | solution.py:205
  23.6 28.9 %collective-permute-start.3 = (bf16[3,128,512]{2,1,0:T(8,128)(2,1)}, bf16[3,128,512]{2,1,0:T(8,128)(2,1)}, u32[]{:S(2)}, u32[]{:S(2)}) collective-permute-start(bf16[3,128,512]{2,1,0:T(8,128)(2,1)} %get-tuple-element.86), channel_id=1, source_target_pairs={{0,3},{1,4},{2,5},{3,6},{4,7},{5,0},{6,1},{7,2},{8,11},{9,12},{10,... | collective-permute-start | bytes 1179656 | tf_op jit(solution)/shard_map/ppermute | solution.py:205
  25.9 27.7 %collective-permute-start.4 = (bf16[3,128,512]{2,1,0:T(8,128)(2,1)}, bf16[3,128,512]{2,1,0:T(8,128)(2,1)}, u32[]{:S(2)}, u32[]{:S(2)}) collective-permute-start(bf16[3,128,512]{2,1,0:T(8,128)(2,1)} %get-tuple-element.87), channel_id=1, source_target_pairs={{0,4},{1,5},{2,6},{3,7},{4,0},{5,1},{6,2},{7,3},{8,12},{9,13},{10,... | collective-permute-start | bytes 1179656 | tf_op jit(solution)/shard_map/ppermute | solution.py:205
  27.7 30.4 %collective-permute-start.5 = (bf16[3,128,512]{2,1,0:T(8,128)(2,1)}, bf16[3,128,512]{2,1,0:T(8,128)(2,1)}, u32[]{:S(2)}, u32[]{:S(2)}) collective-permute-start(bf16[3,128,512]{2,1,0:T(8,128)(2,1)} %get-tuple-element.88), channel_id=1, source_target_pairs={{0,5},{1,6},{2,7},{3,0},{4,1},{5,2},{6,3},{7,4},{8,13},{9,14},{10,... | collective-permute-start | bytes 1179656 | tf_op jit(solution)/shard_map/ppermute | solution.py:205
  34.4 23.8 %collective-permute-start.6 = (bf16[3,128,512]{2,1,0:T(8,128)(2,1)}, bf16[3,128,512]{2,1,0:T(8,128)(2,1)}, u32[]{:S(2)}, u32[]{:S(2)}) collective-permute-start(bf16[3,128,512]{2,1,0:T(8,128)(2,1)} %get-tuple-element.89), channel_id=1, source_target_pairs={{0,6},{1,7},{2,0},{3,1},{4,2},{5,3},{6,4},{7,5},{8,14},{9,15},{10,... | collective-permute-start | bytes 1179656 | tf_op jit(solution)/shard_map/ppermute | solution.py:205
  36.2 23.9 %collective-permute-start.7 = (bf16[3,128,512]{2,1,0:T(8,128)(2,1)}, bf16[3,128,512]{2,1,0:T(8,128)(2,1)}, u32[]{:S(2)}, u32[]{:S(2)}) collective-permute-start(bf16[3,128,512]{2,1,0:T(8,128)(2,1)} %get-tuple-element.90), channel_id=1, source_target_pairs={{0,7},{1,0},{2,1},{3,2},{4,3},{5,4},{6,5},{7,6},{8,15},{9,8},{10,9... | collective-permute-start | bytes 1179656 | tf_op jit(solution)/shard_map/ppermute | solution.py:205
  73.6 29.5 %copy-start.24 = (bf16[4,128,128]{2,1,0:T(8,128)(2,1)S(1)}, bf16[4,128,128]{2,1,0:T(8,128)(2,1)}, u32[]{:S(2)}) copy-start(bf16[4,128,128]{2,1,0:T(8,128)(2,1)} %get-tuple-element.116) | copy-start | bytes 393220
  73.6 40.0 %all-to-all-start.1 = ((bf16[32,10,32,128]{3,2,1,0:T(8,128)(2,1)}), bf16[32,10,32,128]{3,2,1,0:T(8,128)(2,1)}, u32[]{:S(2)}, u32[]{:S(2)}) async-start(bf16[32,10,32,128]{3,2,1,0:T(8,128)(2,1)} %shard_map.86), calls=%async_computation.1 | async-start | bytes 5242880 | tf_op jit(solution)/shard_map/all_to_all | solution.py:258
  81.8 21.2 %collective-permute-start.15 = (bf16[4,4,144,128]{3,2,1,0:T(8,128)(2,1)}, bf16[4,4,144,128]{3,2,1,0:T(8,128)(2,1)S(1)}, u32[]{:S(2)}, u32[]{:S(2)}) collective-permute-start(bf16[4,4,144,128]{3,2,1,0:T(8,128)(2,1)} %get-tuple-element.123), channel_id=1, source_target_pairs={{0,1},{1,0},{2,3},{3,2},{4,5},{5,4},{6,7},{7,6},{8,9},{9,8},{10,11... | collective-permute-start | bytes 1769480 | tf_op jit(solution)/shard_map/ppermute | solution.py:205
  82.1 13.9 %collective-permute-start.10 = (bf16[4,128,128]{2,1,0:T(8,128)(2,1)S(1)}, bf16[4,128,128]{2,1,0:T(8,128)(2,1)S(1)}, u32[]{:S(2)}, u32[]{:S(2)}) collective-permute-start(bf16[4,128,128]{2,1,0:T(8,128)(2,1)S(1)} %copy-done.28), channel_id=1, source_target_pairs={{0,96},{32,128},{64,160},{96,192},{128,224},{160,0},{192,32},{224,... | collective-permute-start | bytes 393224 | tf_op jit(solution)/shard_map/ppermute | solution.py:205
  85.4 14.5 %collective-permute-start.11 = (bf16[4,128,128]{2,1,0:T(8,128)(2,1)S(1)}, bf16[4,128,128]{2,1,0:T(8,128)(2,1)S(1)}, u32[]{:S(2)}, u32[]{:S(2)}) collective-permute-start(bf16[4,128,128]{2,1,0:T(8,128)(2,1)S(1)} %copy-done.26), channel_id=1, source_target_pairs={{0,128},{32,160},{64,192},{96,224},{128,0},{160,32},{192,64},{224,... | collective-permute-start | bytes 393224 | tf_op jit(solution)/shard_map/ppermute | solution.py:205
  88.1 20.3 %collective-permute-start.12 = (bf16[4,128,128]{2,1,0:T(8,128)(2,1)}, bf16[4,128,128]{2,1,0:T(8,128)(2,1)S(1)}, u32[]{:S(2)}, u32[]{:S(2)}) collective-permute-start(bf16[4,128,128]{2,1,0:T(8,128)(2,1)} %get-tuple-element.119), channel_id=1, source_target_pairs={{0,160},{32,192},{64,224},{96,0},{128,32},{160,64},{192,96},{224,1... | collective-permute-start | bytes 393224 | tf_op jit(solution)/shard_map/ppermute | solution.py:205
  92.5 18.3 %collective-permute-start.13 = (bf16[4,128,128]{2,1,0:T(8,128)(2,1)}, bf16[4,128,128]{2,1,0:T(8,128)(2,1)S(1)}, u32[]{:S(2)}, u32[]{:S(2)}) collective-permute-start(bf16[4,128,128]{2,1,0:T(8,128)(2,1)} %get-tuple-element.120), channel_id=1, source_target_pairs={{0,192},{32,224},{64,0},{96,32},{128,64},{160,96},{192,128},{224,1... | collective-permute-start | bytes 393224 | tf_op jit(solution)/shard_map/ppermute | solution.py:205
  96.0 15.8 %collective-permute-start.14 = (bf16[4,128,128]{2,1,0:T(8,128)(2,1)}, bf16[4,128,128]{2,1,0:T(8,128)(2,1)S(1)}, u32[]{:S(2)}, u32[]{:S(2)}) collective-permute-start(bf16[4,128,128]{2,1,0:T(8,128)(2,1)} %get-tuple-element.121), channel_id=1, source_target_pairs={{0,224},{32,0},{64,32},{96,64},{128,96},{160,128},{192,160},{224,1... | collective-permute-start | bytes 393224 | tf_op jit(solution)/shard_map/ppermute | solution.py:205
  99.9 11.8 %collective-permute-start.8 = (bf16[4,128,128]{2,1,0:T(8,128)(2,1)S(1)}, bf16[4,128,128]{2,1,0:T(8,128)(2,1)S(1)}, u32[]{:S(2)}, u32[]{:S(2)}) collective-permute-start(bf16[4,128,128]{2,1,0:T(8,128)(2,1)S(1)} %copy-done.25), channel_id=1, source_target_pairs={{0,32},{32,64},{64,96},{96,128},{128,160},{160,192},{192,224},{224... | collective-permute-start | bytes 393224 | tf_op jit(solution)/shard_map/ppermute | solution.py:205
  103.1 9.8 %collective-permute-start.9 = (bf16[4,128,128]{2,1,0:T(8,128)(2,1)S(1)}, bf16[4,128,128]{2,1,0:T(8,128)(2,1)S(1)}, u32[]{:S(2)}, u32[]{:S(2)}) collective-permute-start(bf16[4,128,128]{2,1,0:T(8,128)(2,1)S(1)} %copy-done.24), channel_id=1, source_target_pairs={{0,64},{32,96},{64,128},{96,160},{128,192},{160,224},{192,0},{224,... | collective-permute-start | bytes 393224 | tf_op jit(solution)/shard_map/ppermute | solution.py:205
  117.7 31.8 %all-to-all-start.2 = ((bf16[32,6,32,128]{3,2,1,0:T(8,128)(2,1)}), bf16[32,6,32,128]{3,2,1,0:T(8,128)(2,1)S(1)}, u32[]{:S(2)}, u32[]{:S(2)}) async-start(bf16[32,6,32,128]{3,2,1,0:T(8,128)(2,1)} %shard_map.87), calls=%async_computation.2 | async-start | bytes 3145728 | tf_op jit(solution)/shard_map/all_to_all | solution.py:258
  125.1 8.6 %collective-permute-start.21 = (bf16[4,128,128]{2,1,0:T(8,128)(2,1)S(1)}, bf16[4,128,128]{2,1,0:T(8,128)(2,1)S(1)}, u32[]{:S(2)}, u32[]{:S(2)}) collective-permute-start(bf16[4,128,128]{2,1,0:T(8,128)(2,1)S(1)} %copy-done.31), channel_id=1, source_target_pairs={{0,64},{32,96},{64,128},{96,160},{128,192},{160,224},{192,0},{224,... | collective-permute-start | bytes 393224 | tf_op jit(solution)/shard_map/ppermute | solution.py:205
  127.2 13.6 %collective-permute-start.17 = (bf16[4,128,128]{2,1,0:T(8,128)(2,1)S(1)}, bf16[4,128,128]{2,1,0:T(8,128)(2,1)S(1)}, u32[]{:S(2)}, u32[]{:S(2)}) collective-permute-start(bf16[4,128,128]{2,1,0:T(8,128)(2,1)S(1)} %copy-done.30), channel_id=1, source_target_pairs={{0,192},{32,224},{64,0},{96,32},{128,64},{160,96},{192,128},{224,1... | collective-permute-start | bytes 393224 | tf_op jit(solution)/shard_map/ppermute | solution.py:205
  129.4 16.9 %collective-permute-start.18 = (bf16[4,128,128]{2,1,0:T(8,128)(2,1)S(1)}, bf16[4,128,128]{2,1,0:T(8,128)(2,1)S(1)}, u32[]{:S(2)}, u32[]{:S(2)}) collective-permute-start(bf16[4,128,128]{2,1,0:T(8,128)(2,1)S(1)} %copy-done.29), channel_id=1, source_target_pairs={{0,160},{32,192},{64,224},{96,0},{128,32},{160,64},{192,96},{224,1... | collective-permute-start | bytes 393224 | tf_op jit(solution)/shard_map/ppermute | solution.py:205
  133.8 32.2 %copy-start.11 = (bf16[4,128,128]{2,1,0:T(8,128)(2,1)}, bf16[4,128,128]{2,1,0:T(8,128)(2,1)S(1)}, u32[]{:S(2)}) copy-start(bf16[4,128,128]{2,1,0:T(8,128)(2,1)S(1)} %collective-permute-done.21.refs_6_) | copy-start | bytes 393220
  133.8 28.9 %collective-permute-start.23 = (bf16[2,4,144,128]{3,2,1,0:T(8,128)(2,1)}, bf16[2,4,144,128]{3,2,1,0:T(8,128)(2,1)S(1)}, u32[]{:S(2)}, u32[]{:S(2)}) collective-permute-start(bf16[2,4,144,128]{3,2,1,0:T(8,128)(2,1)} %get-tuple-element.158), channel_id=1, source_target_pairs={{0,2},{2,4},{4,6},{6,0},{1,3},{3,5},{5,7},{7,1},{8,10},{10,12},{12... | collective-permute-start | bytes 884744 | tf_op jit(solution)/shard_map/ppermute | solution.py:205
  135.3 27.5 %collective-permute-start.24 = (bf16[2,4,144,128]{3,2,1,0:T(8,128)(2,1)}, bf16[2,4,144,128]{3,2,1,0:T(8,128)(2,1)S(1)}, u32[]{:S(2)}, u32[]{:S(2)}) collective-permute-start(bf16[2,4,144,128]{3,2,1,0:T(8,128)(2,1)} %get-tuple-element.159), channel_id=1, source_target_pairs={{0,4},{2,6},{4,0},{6,2},{1,5},{3,7},{5,1},{7,3},{8,12},{10,14},{12... | collective-permute-start | bytes 884744 | tf_op jit(solution)/shard_map/ppermute | solution.py:205
  138.0 24.8 %collective-permute-start.25 = (bf16[2,4,144,128]{3,2,1,0:T(8,128)(2,1)S(1)}, bf16[2,4,144,128]{3,2,1,0:T(8,128)(2,1)S(1)}, u32[]{:S(2)}, u32[]{:S(2)}) collective-permute-start(bf16[2,4,144,128]{3,2,1,0:T(8,128)(2,1)S(1)} %copy-done.23), channel_id=1, source_target_pairs={{0,6},{2,0},{4,2},{6,4},{1,7},{3,1},{5,3},{7,5},{8,14},{10,8},{12,... | collective-permute-start | bytes 884744 | tf_op jit(solution)/shard_map/ppermute | solution.py:205
  140.7 13.4 %collective-permute-start.19 = (bf16[4,128,128]{2,1,0:T(8,128)(2,1)}, bf16[4,128,128]{2,1,0:T(8,128)(2,1)S(1)}, u32[]{:S(2)}, u32[]{:S(2)}) collective-permute-start(bf16[4,128,128]{2,1,0:T(8,128)(2,1)} %get-tuple-element.148), channel_id=1, source_target_pairs={{0,128},{32,160},{64,192},{96,224},{128,0},{160,32},{192,64},{224,... | collective-permute-start | bytes 393224 | tf_op jit(solution)/shard_map/ppermute | solution.py:205
  146.3 12.9 %collective-permute-start.20 = (bf16[4,128,128]{2,1,0:T(8,128)(2,1)S(1)}, bf16[4,128,128]{2,1,0:T(8,128)(2,1)S(1)}, u32[]{:S(2)}, u32[]{:S(2)}) collective-permute-start(bf16[4,128,128]{2,1,0:T(8,128)(2,1)S(1)} %copy-done.27), channel_id=1, source_target_pairs={{0,96},{32,128},{64,160},{96,192},{128,224},{160,0},{192,32},{224,... | collective-permute-start | bytes 393224 | tf_op jit(solution)/shard_map/ppermute | solution.py:205
  154.1 8.6 %collective-permute-start.16 = (bf16[4,128,128]{2,1,0:T(8,128)(2,1)}, bf16[4,128,128]{2,1,0:T(8,128)(2,1)S(1)}, u32[]{:S(2)}, u32[]{:S(2)}) collective-permute-start(bf16[4,128,128]{2,1,0:T(8,128)(2,1)} %get-tuple-element.145), channel_id=1, source_target_pairs={{0,224},{32,0},{64,32},{96,64},{128,96},{160,128},{192,160},{224,1... | collective-permute-start | bytes 393224 | tf_op jit(solution)/shard_map/ppermute | solution.py:205
  159.1 6.8 %collective-permute-start.22 = (bf16[4,128,128]{2,1,0:T(8,128)(2,1)}, bf16[4,128,128]{2,1,0:T(8,128)(2,1)S(1)}, u32[]{:S(2)}, u32[]{:S(2)}) collective-permute-start(bf16[4,128,128]{2,1,0:T(8,128)(2,1)} %get-tuple-element.156), channel_id=1, source_target_pairs={{0,32},{32,64},{64,96},{96,128},{128,160},{160,192},{192,224},{224... | collective-permute-start | bytes 393224 | tf_op jit(solution)/shard_map/ppermute | solution.py:205
  (29 other events, 284.3 us)
